TPU v7x, 512 devices: a whole 4x4x16 slice. The times are simulated.
512 devices in a mesh: blk: 128 (over z, y, core), uly: 4 (over x).
Axes of the slice: x: 4, y: 4, z: 16, core: 2. Of those that a mesh axis runs over, the one named last changes fastest.
Arguments:
- queries: bfloat16 [65536, 2048], P(('blk', 'uly')), may hold values from -10 to 10
- keys: bfloat16 [65536, 512], P(('blk', 'uly')), may hold values from -8 to 8
- values: bfloat16 [65536, 512], P(('blk', 'uly')), may hold values from -6 to 6
- out_grad: bfloat16 [65536, 2048], P(('blk', 'uly')), may hold values from -6 to 6
- docs: int32 [65536], P(('blk', 'uly')), may hold values from 0 to 126, never falling along the last dimension, each value on 1 to 1025 neighbouring positions
Outputs:
- attended: bfloat16 [65536, 2048], P(('blk', 'uly'))
- query_grad: float32 [65536, 2048], P(('blk', 'uly'))
- key_grad: float32 [65536, 512], P(('blk', 'uly'))
- value_grad: float32 [65536, 512], P(('blk', 'uly'))
Inputs may be any that keep to these rules, and one draw needn't show every extreme that they name: `docs`: document ids never fall along the sequence; each document holds 1 to 1025 consecutive tokens, and one holds exactly 1025.
All inputs are finite; a program needn't handle non-finite values.
Results may differ from a plain program's by a relative error of at most 0.038.
Values may be sent and summed in bfloat16 or wider, within the bound.
A program may use at most 64 MiB of HBM per device.

v0:
```python
from functools import partial

import jax
import jax.numpy as jnp
from jax import lax
from jax.sharding import PartitionSpec as P

HD = 128
KVH = 4
GQ = 4
GROUP = 3


def passed_along(block, axis, distance):
    devices = range(lax.axis_size(axis))
    route = [(i - distance, i) for i in devices if i - distance in devices]
    return lax.ppermute(block, axis, route)


def on_device(queries, keys, values, out_grad, docs):
    tokens = queries.shape[0]
    cycle_place = lax.axis_index("blk")
    lanes = lax.axis_size("uly")
    span = tokens * lanes
    scale = HD ** (-0.5)
    own_docs = docs.astype(jnp.bfloat16)
    key_base = jnp.arange(span, dtype=jnp.int32)
    doc_cols = jnp.broadcast_to(own_docs[:, None], (tokens, KVH))
    key_rows, value_rows, doc_rows = (
        lax.all_to_all(keys, "uly", split_axis=1, concat_axis=0, tiled=True),
        lax.all_to_all(values, "uly", split_axis=1, concat_axis=0, tiled=True),
        lax.all_to_all(doc_cols, "uly", split_axis=1, concat_axis=0, tiled=True),
    )
    key_blk = key_rows[None]
    value_blk = value_rows[None]
    block_docs = doc_rows[:, 0]
    query_heads, grad_heads = (
        lax.all_to_all(queries, "uly", split_axis=1, concat_axis=0, tiled=True),
        lax.all_to_all(out_grad, "uly", split_axis=1, concat_axis=0, tiled=True),
    )
    rows_query = query_heads.reshape(span, GQ, HD).transpose(1, 0, 2).reshape(1, GQ * span, HD)
    rows_grad = grad_heads.reshape(span, GQ, HD).transpose(1, 0, 2).reshape(1, GQ * span, HD)
    row_place = jnp.tile(cycle_place * span + key_base, GQ)
    row_doc = jnp.tile(block_docs, GQ)
    groups = rows_query.shape[0]
    row_count = rows_query.shape[1]
    local_block = (key_blk, value_blk, block_docs)
    blocks = [local_block]
    moving = local_block
    for offset in range(1, GROUP):
        moving = passed_along((moving[0], moving[1], moving[2]), "blk", 1)
        blocks.append(moving)

    def block_scores(block, offset):
        key_part_blk, value_part_blk, doc_part = block
        key_place = (cycle_place - offset) * span + key_base
        scores = (
            jnp.einsum("grd,gkd->grk", rows_query, key_part_blk, preferred_element_type=jnp.float32)
            * scale
        )
        allowed = (key_place[None, :] <= row_place[:, None]) & (
            doc_part[None, :] == row_doc[:, None]
        )
        return (scores, allowed[None])

    def forward_tile(state, block, offset):
        top, total, summed = state
        scores, allowed = block_scores(block, offset)
        scores = jnp.where(allowed, scores, -jnp.inf)
        new_top = jnp.maximum(top, jnp.max(scores, axis=2, keepdims=True))
        factor = jnp.exp(top - new_top)
        shifted = jnp.exp(scores - new_top)
        total = total * factor + jnp.sum(shifted, axis=2, keepdims=True)
        summed = summed * factor + jnp.einsum(
            "grk,gkd->grd",
            shifted.astype(jnp.bfloat16),
            block[1],
            preferred_element_type=jnp.float32,
        )
        return (new_top, total, summed)

    def keep_state(state):
        return state

    state = (
        jnp.full((groups, row_count, 1), -jnp.inf, jnp.float32),
        jnp.zeros((groups, row_count, 1), jnp.float32),
        jnp.zeros((groups, row_count, HD), jnp.float32),
    )
    state = forward_tile(state, blocks[0], 0)
    for offset in range(1, GROUP):
        state = lax.cond(
            offset <= cycle_place,
            partial(forward_tile, block=blocks[offset], offset=offset),
            keep_state,
            state,
        )
    top, total, summed = state
    lse = top + jnp.log(total)
    attended_rows = (summed / total).astype(jnp.bfloat16)
    delta = jnp.sum(
        rows_grad.astype(jnp.float32) * attended_rows.astype(jnp.float32), axis=2, keepdims=True
    )

    def backward_tile(block, offset):
        scores, allowed = block_scores(block, offset)
        probs = jnp.where(allowed, jnp.exp(scores - lse), 0.0)
        value_part = jnp.einsum(
            "grk,grd->gkd",
            probs.astype(jnp.bfloat16),
            rows_grad,
            preferred_element_type=jnp.float32,
        )
        dprob = jnp.einsum("grd,gkd->grk", rows_grad, block[1], preferred_element_type=jnp.float32)
        dscore = (probs * (dprob - delta)).astype(jnp.bfloat16)
        query_part = (
            jnp.einsum("grk,gkd->grd", dscore, block[0], preferred_element_type=jnp.float32) * scale
        )
        key_part = (
            jnp.einsum("grk,grd->gkd", dscore, rows_query, preferred_element_type=jnp.float32)
            * scale
        )
        pair_part = (
            jnp.stack([key_part, value_part]).transpose(0, 2, 1, 3).reshape(2, span, groups * HD)
        )
        return (query_part, pair_part)

    def empty_tile():
        return (
            jnp.zeros((groups, row_count, HD), jnp.float32),
            jnp.zeros((2, span, groups * HD), jnp.float32),
        )

    def tile_terms(offset):
        if offset == 0:
            return backward_tile(blocks[0], 0)
        return lax.cond(
            offset <= cycle_place, partial(backward_tile, blocks[offset], offset), empty_tile
        )

    query_rows_grad = jnp.zeros((groups, row_count, HD), jnp.float32)
    carried = jnp.zeros((2, span, groups * HD), jnp.float32)
    for step in range(GROUP):
        query_part, pair_part = tile_terms(GROUP - 1 - step)
        query_rows_grad = query_rows_grad + query_part
        carried = carried + pair_part
        if step < GROUP - 1:
            carried = passed_along(carried.astype(jnp.bfloat16), "blk", -1).astype(carried.dtype)
    pair_home = lax.all_to_all(
        carried.astype(jnp.bfloat16), "uly", split_axis=1, concat_axis=2, tiled=True
    ).astype(carried.dtype)
    attended_cols = attended_rows.reshape(GQ, span, HD).transpose(1, 0, 2).reshape(span, GQ * HD)
    query_cols = query_rows_grad.reshape(GQ, span, HD).transpose(1, 0, 2).reshape(span, GQ * HD)
    attended = lax.all_to_all(attended_cols, "uly", split_axis=0, concat_axis=1, tiled=True)
    query_grad = lax.all_to_all(
        query_cols.astype(jnp.bfloat16), "uly", split_axis=0, concat_axis=1, tiled=True
    ).astype(query_cols.dtype)
    return (attended, query_grad, pair_home[0], pair_home[1])


def solution(mesh):
    return jax.shard_map(
        on_device,
        mesh=mesh,
        in_specs=(
            P(("blk", "uly"), None),
            P(("blk", "uly"), None),
            P(("blk", "uly"), None),
            P(("blk", "uly"), None),
            P(("blk", "uly")),
        ),
        out_specs=(
            P(("blk", "uly"), None),
            P(("blk", "uly"), None),
            P(("blk", "uly"), None),
            P(("blk", "uly"), None),
        ),
        check_vma=False,
    )
```

profile of v0, /device:TPU:384, one launch (start us, length us, event | category | flops | bytes accessed | tf_op | source)
XLA Modules:
  0.0 147.3 jit_solution(18431388549073092678)
XLA Ops:
  1.9 4.3 %all-to-all-start = ((bf16[128,4,1]{0,2,1:T(2,128)(2,1)}), bf16[128,4,1]{0,2,1:T(2,128)(2,1)S(1)}, u32[]{:S(2)}, u32[]{:S(2)}) async-start(bf16[128,4,1]{0,2,1:T(2,128)(2,1)} %broadcast_in_dim.74), calls=%async_computation | async-start | bytes 4096 | tf_op jit(solution)/shard_map/all_to_all | solution.py:32
  6.9 4.5 %all-to-all-done = bf16[128,4,1]{0,2,1:T(2,128)(2,1)S(1)} async-done(((bf16[128,4,1]{0,2,1:T(2,128)(2,1)}), bf16[128,4,1]{0,2,1:T(2,128)(2,1)S(1)}, u32[]{:S(2)}, u32[]{:S(2)}) %all-to-all-start) | async-done | bytes 1056 | tf_op jit(solution)/shard_map/all_to_all | solution.py:32
  11.4 3.3 %all-to-all-start.2 = ((bf16[128,4,128]{2,0,1:T(8,128)(2,1)}), bf16[128,4,128]{2,0,1:T(8,128)(2,1)S(1)}, u32[]{:S(2)}, u32[]{:S(2)}) async-start(bf16[128,4,128]{2,0,1:T(8,128)(2,1)} %copy_bitcast_fusion.7), calls=%async_computation.2 | async-start | bytes 262144 | tf_op jit(solution)/shard_map/all_to_all | solution.py:30
  18.2 2.5 %all-to-all-done.2 = bf16[128,4,128]{2,0,1:T(8,128)(2,1)S(1)} async-done(((bf16[128,4,128]{2,0,1:T(8,128)(2,1)}), bf16[128,4,128]{2,0,1:T(8,128)(2,1)S(1)}, u32[]{:S(2)}, u32[]{:S(2)}) %all-to-all-start.2) | async-done | bytes 131104 | tf_op jit(solution)/shard_map/all_to_all | solution.py:30
  20.7 3.3 %all-to-all-start.3 = ((bf16[128,4,128]{2,0,1:T(8,128)(2,1)}), bf16[128,4,128]{2,0,1:T(8,128)(2,1)S(1)}, u32[]{:S(2)}, u32[]{:S(2)}) async-start(bf16[128,4,128]{2,0,1:T(8,128)(2,1)} %copy_bitcast_fusion.6), calls=%async_computation.3 | async-start | bytes 262144 | tf_op jit(solution)/shard_map/all_to_all | solution.py:31
  24.0 5.9 %all-to-all-done.3 = bf16[128,4,128]{2,0,1:T(8,128)(2,1)S(1)} async-done(((bf16[128,4,128]{2,0,1:T(8,128)(2,1)}), bf16[128,4,128]{2,0,1:T(8,128)(2,1)S(1)}, u32[]{:S(2)}, u32[]{:S(2)}) %all-to-all-start.3) | async-done | bytes 131104 | tf_op jit(solution)/shard_map/all_to_all | solution.py:31
  30.0 3.5 %all-to-all-start.1 = ((bf16[128,4,512]{2,0,1:T(8,128)(2,1)}), bf16[128,4,512]{2,0,1:T(8,128)(2,1)S(1)}, u32[]{:S(2)}, u32[]{:S(2)}) async-start(bf16[128,4,512]{2,0,1:T(8,128)(2,1)} %bitcast.223), calls=%async_computation.1 | async-start | bytes 1048576 | tf_op jit(solution)/shard_map/all_to_all | solution.py:38
  35.4 1.9 %collective-permute-start = (bf16[512]{0:T(512)(128)(2,1)S(1)}, bf16[512]{0:T(512)(128)(2,1)}, u32[]{:S(2)}, u32[]{:S(2)}) collective-permute-start(bf16[512]{0:T(512)(128)(2,1)S(1)} %bitcast.294), channel_id=1, source_target_pairs={{0,4},{4,8},{8,12},{12,16},{16,20},{20,24},{24,28},{28,32},{32,36}... | collective-permute-start | bytes 3080 | tf_op jit(solution)/shard_map/ppermute | solution.py:17
  37.3 3.6 %collective-permute-start.2 = (bf16[1,512,128]{2,1,0:T(8,128)(2,1)S(1)}, bf16[1,512,128]{2,1,0:T(8,128)(2,1)S(1)}, u32[]{:S(2)}, u32[]{:S(2)}) collective-permute-start(bf16[1,512,128]{2,1,0:T(8,128)(2,1)S(1)} %bitcast.268), channel_id=1, source_target_pairs={{0,4},{4,8},{8,12},{12,16},{16,20},{20,24},{24,28},{28,32},{32,36}... | collective-permute-start | bytes 393224 | tf_op jit(solution)/shard_map/ppermute | solution.py:17
  43.7 2.8 %collective-permute-start.3 = (bf16[512]{0:T(512)(128)(2,1)}, bf16[512]{0:T(512)(128)(2,1)}, u32[]{:S(2)}, u32[]{:S(2)}) collective-permute-start(bf16[512]{0:T(512)(128)(2,1)} %collective-permute-done), channel_id=1, source_target_pairs={{0,4},{4,8},{8,12},{12,16},{16,20},{20,24},{24,28},{28,32},{32,36}... | collective-permute-start | bytes 3080 | tf_op jit(solution)/shard_map/ppermute | solution.py:17
  52.6 4.7 %all-to-all-start.5 = ((bf16[128,4,512]{2,0,1:T(8,128)(2,1)}), bf16[128,4,512]{2,0,1:T(8,128)(2,1)S(1)}, u32[]{:S(2)}, u32[]{:S(2)}) async-start(bf16[128,4,512]{2,0,1:T(8,128)(2,1)} %bitcast.222), calls=%async_computation.5 | async-start | bytes 1048576 | tf_op jit(solution)/shard_map/all_to_all | solution.py:39
  61.9 4.3 %all-to-all-done.5 = bf16[128,4,512]{2,0,1:T(8,128)(2,1)S(1)} async-done(((bf16[128,4,512]{2,0,1:T(8,128)(2,1)}), bf16[128,4,512]{2,0,1:T(8,128)(2,1)S(1)}, u32[]{:S(2)}, u32[]{:S(2)}) %all-to-all-start.5) | async-done | bytes 524320 | tf_op jit(solution)/shard_map/all_to_all | solution.py:39
  66.4 3.8 %conditional.4 = ((f32[1,2048,1]{1,2,0:T(1,128)S(1)}, f32[1,2048,1]{1,2,0:T(1,128)S(1)}, f32[1,2048,128]{2,1,0:T(8,128)S(1)})) conditional(s32[]{:T(128)} %convert_element_type.112, (f32[1,2048,1]{1,2,0:T(1,128)S(1)}, f32[1,2048,1]{1,2,0:T(1,128)S(1)}, f32[1,2048,128]{2,1,0:T(8,128)S(1)}) %tuple.80, (s32[]{:T(128)}, s32[512]{0:T(512)S(1)}, ...), branch_computations={%region_2.3_spmd, %region_3.6_spmd} | conditional | flops 549982720 | bytes 15641660 | solution.py:92
  66.4 1.9 %fusion.64 = (f32[2048]{0:T(1024)S(1)}, f32[2048,512]{0,1:T(8,128)S(1)}) fusion(bf16[1,512,128]{2,1,0:T(8,128)(2,1)} %get-tuple-element.107, bf16[1,2048,128]{2,1,0:T(8,128)(2,1)S(1)} %get-tuple-element.106, bf16[2048]{0:T(1024)(128)(2,1)S(1)} %bitcast.312, bf16[512]{0:T(512)(128)(2,1)} %get-tuple-element.104, s32[2048]{0:T(1024)S(1)} %bitcast.308, ...), kind=kOutput, calls=%fused_computation.109 | convolution fusion | flops 276822016 | bytes 4873216 | tf_op jit(solution)/shard_map/cond/branch_1_fun/grd,gkd->grk/dot_general | solution.py:58
  70.2 3.8 %conditional.5 = (f32[1,2048,1]{1,2,0:T(1,128)S(1)}, f32[1,2048,128]{2,1,0:T(8,128)S(1)}, f32[1,2048,1]{1,2,0:T(1,128)S(1)}) conditional(s32[]{:T(128)} %convert_element_type.111, (f32[1,2048,1]{1,2,0:T(1,128)S(1)}, f32[1,2048,1]{1,2,0:T(1,128)S(1)}, f32[1,2048,128]{2,1,0:T(8,128)S(1)}) %get-tuple-element.238, (s32[]{:T(128)}, ...), branch_computations={%region_6.7_spmd.clone, %region_7.10_spmd.clone} | conditional | flops 549984768 | bytes 15633460 | solution.py:92
  70.3 1.9 %fusion.65 = (f32[2048]{0:T(1024)S(1)}, f32[2048,512]{0,1:T(8,128)S(1)}) fusion(bf16[1,512,128]{2,1,0:T(8,128)(2,1)} %get-tuple-element.194, bf16[1,2048,128]{2,1,0:T(8,128)(2,1)S(1)} %get-tuple-element.193, bf16[2048]{0:T(1024)(128)(2,1)S(1)} %bitcast.313, bf16[512]{0:T(512)(128)(2,1)} %get-tuple-element.191, s32[2048]{0:T(1024)S(1)} %bitcast.309, ...), kind=kOutput, calls=%fused_computation.110 | convolution fusion | flops 276822016 | bytes 4873216 | tf_op jit(solution)/shard_map/cond/branch_1_fun/grd,gkd->grk/dot_general | solution.py:58
  76.7 4.3 %all-to-all-start.4 = ((bf16[4,128,512]{2,1,0:T(8,128)(2,1)}), bf16[4,128,512]{2,1,0:T(8,128)(2,1)}, u32[]{:S(2)}, u32[]{:S(2)}) async-start(bf16[4,128,512]{2,1,0:T(8,128)(2,1)} %all_to_all.98), calls=%async_computation.4 | async-start | bytes 1048576 | tf_op jit(solution)/shard_map/all_to_all | solution.py:154
  81.1 3.8 %multiply_convert_fusion.2 = bf16[2048,512]{0,1:T(8,128)(2,1)S(1)} fusion(bf16[2048,128]{1,0:T(8,128)(2,1)S(1)} %bitcast.228, bf16[512,128]{1,0:T(8,128)(2,1)} %bitcast.270, f32[2048,512]{0,1:T(8,128)} %copy-done.1, f32[2048]{0:T(1024)} %get-tuple-element.206, f32[2048]{0:T(1024)} %bitcast.304, s32[2048]{0:T(1024)} %bitcast.285, s32[512]{0:T(512)S(1)} %iota_add_fusion, ...), kind=kOutput, calls=%fused_computation.64 | convolution fusion | flops 279969792 | bytes 6978560 | tf_op jit(solution)/shard_map/grd,gkd->grk/dot_general | solution.py:114
  87.2 8.6 %conditional.6 = (f32[1,2048,128]{2,1,0:T(8,128)}, bf16[2,512,128]{2,1,0:T(8,128)(2,1)}) conditional(s32[]{:T(128)} %convert_element_type.111, () %tuple.40, (s32[]{:T(128)}, s32[512]{0:T(512)}, s32[4,512]{1,0:T(4,128)S(1)}, bf16[512]{0:T(512)(128)(2,1)}, bf16[4,512]{1,0:T(4,128)(2,1)S(1)}, /*index=5*/bf16[1,2048,128]{2,1,0:T(8,128)(2,1)S(1)}, ...), branch_computations={%region_11.12_spmd, %region_12.13_spmd} | conditional | flops 1355284992 | bytes 23293000 | solution.py:137
  87.9 2.3 %exponential_select_fusion = f32[2048,512]{1,0:T(8,128)S(1)} fusion(f32[2048]{0:T(1024)} %bitcast.306, s32[512]{0:T(512)S(1)} %broadcast_add_fusion.1, s32[2048]{0:T(1024)S(1)} %bitcast.310, bf16[512]{0:T(512)(128)(2,1)} %get-tuple-element.125, bf16[2048]{0:T(1024)(128)(2,1)S(1)} %bitcast.314, bf16[1,2048,128]{2,1,0:T(8,128)(2,1)S(1)} %get-tuple-element.127, ...), kind=kOutput, calls=%fused_computation.14 | convolution fusion | flops 276824064 | bytes 4873216 | tf_op jit(solution)/shard_map/cond/branch_1_fun/grd,gkd->grk/dot_general | solution.py:58
  92.5 2.7 %fusion.8 = f32[1,2048,128]{2,1,0:T(8,128)} fusion(bf16[2048,512]{1,0:T(8,128)(2,1)S(1)} %multiply_convert_fusion, bf16[1,512,128]{2,1,0:T(8,128)(2,1)} %get-tuple-element.128), kind=kOutput, calls=%fused_computation.16 | convolution fusion | flops 268697600 | bytes 3276800 | tf_op jit(solution)/shard_map/cond/branch_1_fun/grk,gkd->grd/dot_general | solution.py:117
  95.8 7.1 %collective-permute-start.6 = (bf16[2,512,128]{2,1,0:T(8,128)(2,1)}, bf16[2,512,128]{2,1,0:T(8,128)(2,1)}, u32[]{:S(2)}, u32[]{:S(2)}) collective-permute-start(bf16[2,512,128]{2,1,0:T(8,128)(2,1)} %get-tuple-element.166), channel_id=1, source_target_pairs={{4,0},{8,4},{12,8},{16,12},{20,16},{24,20},{28,24},{32,28},{36,32}... | collective-permute-start | bytes 786440 | tf_op jit(solution)/shard_map/ppermute | solution.py:17
  102.9 7.2 %conditional.7 = (f32[1,2048,128]{2,1,0:T(8,128)}, f32[2,512,128]{2,1,0:T(8,128)S(1)}) conditional(s32[]{:T(128)} %convert_element_type.112, () %tuple.42, (s32[]{:T(128)}, s32[512]{0:T(512)S(1)}, s32[4,512]{1,0:T(4,128)S(1)}, bf16[512]{0:T(512)(128)(2,1)}, bf16[4,512]{1,0:T(4,128)(2,1)S(1)}, /*index=5*/bf16[1,2048,128]{2,1,0:T(8,128)(2,1)S(1)}, ...), branch_computations={%region_13.14_spmd, %region_14.15_spmd} | conditional | flops 1355219456 | bytes 24079432 | solution.py:137
  103.0 2.3 %exponential_select_fusion.1 = f32[2048,512]{1,0:T(8,128)S(1)} fusion(f32[2048]{0:T(1024)} %bitcast.307, s32[512]{0:T(512)S(1)} %broadcast_add_fusion.2, s32[2048]{0:T(1024)S(1)} %bitcast.311, bf16[512]{0:T(512)(128)(2,1)} %get-tuple-element.136, bf16[2048]{0:T(1024)(128)(2,1)S(1)} %bitcast.315, bf16[1,2048,128]{2,1,0:T(8,128)(2,1)S(1)} %get-tuple-element.138, ...), kind=kOutput, calls=%fused_computation.32 | convolution fusion | flops 276824064 | bytes 4873216 | tf_op jit(solution)/shard_map/cond/branch_1_fun/grd,gkd->grk/dot_general | solution.py:58
  107.5 2.6 %fusion.22 = f32[1,2048,128]{2,1,0:T(8,128)} fusion(bf16[2048,512]{1,0:T(8,128)(2,1)S(1)} %multiply_convert_fusion.1, bf16[1,512,128]{2,1,0:T(8,128)(2,1)} %get-tuple-element.139), kind=kOutput, calls=%fused_computation.34 | convolution fusion | flops 268697600 | bytes 3276800 | tf_op jit(solution)/shard_map/cond/branch_1_fun/grk,gkd->grd/dot_general | solution.py:117
  110.9 2.6 %add_convert_fusion = bf16[1,2048,128]{2,1,0:T(8,128)(2,1)S(1)} fusion(f32[1,2048,128]{2,1,0:T(8,128)} %fusion.46, f32[1,2048,128]{2,1,0:T(8,128)} %get-tuple-element.164, f32[1,2048,128]{2,1,0:T(8,128)} %get-tuple-element.165), kind=kLoop, calls=%fused_computation.82 | loop fusion | flops 786432 | bytes 3670016 | tf_op jit(solution)/shard_map/convert_element_type | solution.py:156
  115.4 2.3 %collective-permute-start.7 = (bf16[2,512,128]{2,1,0:T(8,128)(2,1)}, bf16[2,512,128]{2,1,0:T(8,128)(2,1)}, u32[]{:S(2)}, u32[]{:S(2)}) collective-permute-start(bf16[2,512,128]{2,1,0:T(8,128)(2,1)} %add_convert_fusion.1), channel_id=1, source_target_pairs={{4,0},{8,4},{12,8},{16,12},{20,16},{24,20},{28,24},{32,28},{36,32}... | collective-permute-start | bytes 786440 | tf_op jit(solution)/shard_map/ppermute | solution.py:17
  117.8 1.9 %fusion.54 = f32[1,1,512,128]{3,2,1,0:T(8,128)} fusion(bf16[2048,128]{1,0:T(8,128)(2,1)S(1)} %bitcast.231, f32[2048,512]{0,1:T(8,128)S(1)} %copy-done.2, f32[2048]{0:T(1024)S(1)} %bitcast.305, s32[2048]{0:T(1024)S(1)} %bitcast.286, s32[512]{0:T(512)S(1)} %iota_add_fusion, bf16[2048]{0:T(1024)(128)(2,1)S(1)} %bitcast.293, bf16[512]{0:T(512)(128)(2,1)S(1)} %bitcast.301), kind=kOutput, calls=%fused_computation.80 | convolution fusion | flops 277872640 | bytes 5004288 | tf_op jit(solution)/shard_map/grk,grd->gkd/dot_general | solution.py:108
  121.1 4.7 %all-to-all-start.6 = ((bf16[4,128,512]{2,1,0:T(8,128)(2,1)}), bf16[4,128,512]{2,1,0:T(8,128)(2,1)S(1)}, u32[]{:S(2)}, u32[]{:S(2)}) async-start(bf16[4,128,512]{2,1,0:T(8,128)(2,1)} %convert_element_type.122), calls=%async_computation.6 | async-start | bytes 1048576 | tf_op jit(solution)/shard_map/all_to_all | solution.py:155
  130.9 4.5 %all-to-all-done.6 = bf16[4,128,512]{2,1,0:T(8,128)(2,1)S(1)} async-done(((bf16[4,128,512]{2,1,0:T(8,128)(2,1)}), bf16[4,128,512]{2,1,0:T(8,128)(2,1)S(1)}, u32[]{:S(2)}, u32[]{:S(2)}) %all-to-all-start.6) | async-done | bytes 524320 | tf_op jit(solution)/shard_map/all_to_all | solution.py:155
  135.5 3.4 %all-to-all-start.7 = ((bf16[2,512,128]{2,0,1:T(2,128)(2,1)}), bf16[2,512,128]{2,0,1:T(2,128)(2,1)S(1)}, u32[]{:S(2)}, u32[]{:S(2)}) async-start(bf16[2,512,128]{2,0,1:T(2,128)(2,1)} %copy.53), calls=%async_computation.7 | async-start | bytes 524288 | tf_op jit(solution)/shard_map/all_to_all | solution.py:149
  140.7 4.9 %all-to-all-done.7 = bf16[2,512,128]{2,0,1:T(2,128)(2,1)S(1)} async-done(((bf16[2,512,128]{2,0,1:T(2,128)(2,1)}), bf16[2,512,128]{2,0,1:T(2,128)(2,1)S(1)}, u32[]{:S(2)}, u32[]{:S(2)}) %all-to-all-start.7) | async-done | bytes 262176 | tf_op jit(solution)/shard_map/all_to_all | solution.py:149
  (123 shorter events, 47.9 us)
Async XLA Ops:
  0.6 5.6 %copy-start = (bf16[128,512]{1,0:T(8,128)(2,1)S(1)}, bf16[128,512]{1,0:T(8,128)(2,1)}, u32[]{:S(2)}) copy-start(bf16[128,512]{1,0:T(8,128)(2,1)} %param.14) | copy-start | bytes 393220
  1.9 9.5 %all-to-all-start = ((bf16[128,4,1]{0,2,1:T(2,128)(2,1)}), bf16[128,4,1]{0,2,1:T(2,128)(2,1)S(1)}, u32[]{:S(2)}, u32[]{:S(2)}) async-start(bf16[128,4,1]{0,2,1:T(2,128)(2,1)} %broadcast_in_dim.74), calls=%async_computation | async-start | bytes 4096 | tf_op jit(solution)/shard_map/all_to_all | solution.py:32
  11.4 9.3 %all-to-all-start.2 = ((bf16[128,4,128]{2,0,1:T(8,128)(2,1)}), bf16[128,4,128]{2,0,1:T(8,128)(2,1)S(1)}, u32[]{:S(2)}, u32[]{:S(2)}) async-start(bf16[128,4,128]{2,0,1:T(8,128)(2,1)} %copy_bitcast_fusion.7), calls=%async_computation.2 | async-start | bytes 262144 | tf_op jit(solution)/shard_map/all_to_all | solution.py:30
  20.7 37.9 %copy-start.4 = (bf16[128,4,128]{2,0,1:T(8,128)(2,1)}, bf16[128,4,128]{2,0,1:T(8,128)(2,1)S(1)}, u32[]{:S(2)}) copy-start(bf16[128,4,128]{2,0,1:T(8,128)(2,1)S(1)} %all-to-all-done.2) | copy-start | bytes 393220
  20.7 9.3 %all-to-all-start.3 = ((bf16[128,4,128]{2,0,1:T(8,128)(2,1)}), bf16[128,4,128]{2,0,1:T(8,128)(2,1)S(1)}, u32[]{:S(2)}, u32[]{:S(2)}) async-start(bf16[128,4,128]{2,0,1:T(8,128)(2,1)} %copy_bitcast_fusion.6), calls=%async_computation.3 | async-start | bytes 262144 | tf_op jit(solution)/shard_map/all_to_all | solution.py:31
  30.0 30.1 %copy-start.6 = (bf16[128,4,128]{2,0,1:T(8,128)(2,1)}, bf16[128,4,128]{2,0,1:T(8,128)(2,1)S(1)}, u32[]{:S(2)}) copy-start(bf16[128,4,128]{2,0,1:T(8,128)(2,1)S(1)} %all-to-all-done.3) | copy-start | bytes 393220
  30.0 22.6 %all-to-all-start.1 = ((bf16[128,4,512]{2,0,1:T(8,128)(2,1)}), bf16[128,4,512]{2,0,1:T(8,128)(2,1)S(1)}, u32[]{:S(2)}, u32[]{:S(2)}) async-start(bf16[128,4,512]{2,0,1:T(8,128)(2,1)} %bitcast.223), calls=%async_computation.1 | async-start | bytes 1048576 | tf_op jit(solution)/shard_map/all_to_all | solution.py:38
  33.5 26.6 %copy-start.9 = (s32[1,4,4,128]{3,1,2,0:T(4,128)}, s32[1,4,4,128]{3,1,2,0:T(4,128)S(1)}, u32[]{:S(2)}) copy-start(s32[1,4,4,128]{3,1,2,0:T(4,128)S(1)} %copy.71) | copy-start | bytes 24580
  35.4 31.0 %copy-start.13 = (bf16[4,128]{1,0:T(4,128)(2,1)}, bf16[4,128]{1,0:T(4,128)(2,1)S(1)}, u32[]{:S(2)}) copy-start(bf16[4,128]{1,0:T(4,128)(2,1)S(1)} %bitcast_reduce_fusion) | copy-start | bytes 3076
  35.4 8.3 %collective-permute-start = (bf16[512]{0:T(512)(128)(2,1)S(1)}, bf16[512]{0:T(512)(128)(2,1)}, u32[]{:S(2)}, u32[]{:S(2)}) collective-permute-start(bf16[512]{0:T(512)(128)(2,1)S(1)} %bitcast.294), channel_id=1, source_target_pairs={{0,4},{4,8},{8,12},{12,16},{16,20},{20,24},{24,28},{28,32},{32,36}... | collective-permute-start | bytes 3080 | tf_op jit(solution)/shard_map/ppermute | solution.py:17
  37.3 9.6 %collective-permute-start.2 = (bf16[1,512,128]{2,1,0:T(8,128)(2,1)S(1)}, bf16[1,512,128]{2,1,0:T(8,128)(2,1)S(1)}, u32[]{:S(2)}, u32[]{:S(2)}) collective-permute-start(bf16[1,512,128]{2,1,0:T(8,128)(2,1)S(1)} %bitcast.268), channel_id=1, source_target_pairs={{0,4},{4,8},{8,12},{12,16},{16,20},{20,24},{24,28},{28,32},{32,36}... | collective-permute-start | bytes 393224 | tf_op jit(solution)/shard_map/ppermute | solution.py:17
  40.9 9.7 %collective-permute-start.1 = (bf16[1,512,128]{2,1,0:T(8,128)(2,1)S(1)}, bf16[1,512,128]{2,1,0:T(8,128)(2,1)}, u32[]{:S(2)}, u32[]{:S(2)}) collective-permute-start(bf16[1,512,128]{2,1,0:T(8,128)(2,1)S(1)} %bitcast.254), channel_id=1, source_target_pairs={{0,4},{4,8},{8,12},{12,16},{16,20},{20,24},{24,28},{28,32},{32,36}... | collective-permute-start | bytes 393224 | tf_op jit(solution)/shard_map/ppermute | solution.py:17
  42.9 17.2 %copy-start.11 = (bf16[1,4,4,128]{3,1,2,0:T(4,128)(2,1)}, bf16[1,4,4,128]{3,1,2,0:T(4,128)(2,1)S(1)}, u32[]{:S(2)}) copy-start(bf16[1,4,4,128]{3,1,2,0:T(4,128)(2,1)S(1)} %copy.72) | copy-start | bytes 12292
  43.7 26.5 %collective-permute-start.3 = (bf16[512]{0:T(512)(128)(2,1)}, bf16[512]{0:T(512)(128)(2,1)}, u32[]{:S(2)}, u32[]{:S(2)}) collective-permute-start(bf16[512]{0:T(512)(128)(2,1)} %collective-permute-done), channel_id=1, source_target_pairs={{0,4},{4,8},{8,12},{12,16},{16,20},{20,24},{24,28},{28,32},{32,36}... | collective-permute-start | bytes 3080 | tf_op jit(solution)/shard_map/ppermute | solution.py:17
  46.9 23.3 %collective-permute-start.5 = (bf16[1,512,128]{2,1,0:T(8,128)(2,1)S(1)}, bf16[1,512,128]{2,1,0:T(8,128)(2,1)S(1)}, u32[]{:S(2)}, u32[]{:S(2)}) collective-permute-start(bf16[1,512,128]{2,1,0:T(8,128)(2,1)S(1)} %collective-permute-done.2), channel_id=1, source_target_pairs={{0,4},{4,8},{8,12},{12,16},{16,20},{20,24},{24,28},{28,32},{32,36}... | collective-permute-start | bytes 393224 | tf_op jit(solution)/shard_map/ppermute | solution.py:17
  50.6 19.6 %collective-permute-start.4 = (bf16[1,512,128]{2,1,0:T(8,128)(2,1)}, bf16[1,512,128]{2,1,0:T(8,128)(2,1)}, u32[]{:S(2)}, u32[]{:S(2)}) collective-permute-start(bf16[1,512,128]{2,1,0:T(8,128)(2,1)} %collective-permute-done.1), channel_id=1, source_target_pairs={{0,4},{4,8},{8,12},{12,16},{16,20},{20,24},{24,28},{28,32},{32,36}... | collective-permute-start | bytes 393224 | tf_op jit(solution)/shard_map/ppermute | solution.py:17
  52.6 13.6 %all-to-all-start.5 = ((bf16[128,4,512]{2,0,1:T(8,128)(2,1)}), bf16[128,4,512]{2,0,1:T(8,128)(2,1)S(1)}, u32[]{:S(2)}, u32[]{:S(2)}) async-start(bf16[128,4,512]{2,0,1:T(8,128)(2,1)} %bitcast.222), calls=%async_computation.5 | async-start | bytes 1048576 | tf_op jit(solution)/shard_map/all_to_all | solution.py:39
  58.6 3.2 %copy-start.1 = (f32[2048,512]{0,1:T(8,128)}, f32[2048,512]{0,1:T(8,128)S(1)}, u32[]{:S(2)}) copy-start(f32[2048,512]{0,1:T(8,128)S(1)} %get-tuple-element.215) | copy-start | bytes 12582916
  74.1 7.0 %copy-start.15 = (f32[1,2048,1]{1,2,0:T(1,128)}, f32[1,2048,1]{1,2,0:T(1,128)S(1)}, u32[]{:S(2)}) copy-start(f32[1,2048,1]{1,2,0:T(1,128)S(1)} %get-tuple-element.180) | copy-start | bytes 24580
  76.7 44.4 %all-to-all-start.4 = ((bf16[4,128,512]{2,1,0:T(8,128)(2,1)}), bf16[4,128,512]{2,1,0:T(8,128)(2,1)}, u32[]{:S(2)}, u32[]{:S(2)}) async-start(bf16[4,128,512]{2,1,0:T(8,128)(2,1)} %all_to_all.98), calls=%async_computation.4 | async-start | bytes 1048576 | tf_op jit(solution)/shard_map/all_to_all | solution.py:154
  81.1 3.8 %copy-start.5 = (bf16[128,4,128]{2,0,1:T(8,128)(2,1)S(1)}, bf16[128,4,128]{2,0,1:T(8,128)(2,1)}, u32[]{:S(2)}) copy-start(bf16[128,4,128]{2,0,1:T(8,128)(2,1)} %copy-done.4) | copy-start | bytes 393220
  90.2 0.8 copy-start.7
  95.8 17.6 %collective-permute-start.6 = (bf16[2,512,128]{2,1,0:T(8,128)(2,1)}, bf16[2,512,128]{2,1,0:T(8,128)(2,1)}, u32[]{:S(2)}, u32[]{:S(2)}) collective-permute-start(bf16[2,512,128]{2,1,0:T(8,128)(2,1)} %get-tuple-element.166), channel_id=1, source_target_pairs={{4,0},{8,4},{12,8},{16,12},{20,16},{24,20},{28,24},{32,28},{36,32}... | collective-permute-start | bytes 786440 | tf_op jit(solution)/shard_map/ppermute | solution.py:17
  110.1 0.8 copy-start.3
  110.1 7.6 %copy-start.2 = (f32[2048,512]{0,1:T(8,128)S(1)}, f32[2048,512]{0,1:T(8,128)}, u32[]{:S(2)}) copy-start(f32[2048,512]{0,1:T(8,128)} %copy-done.1) | copy-start | bytes 12582916
  110.1 7.6 %copy-start.10 = (s32[1,4,4,128]{3,1,2,0:T(4,128)S(1)}, s32[1,4,4,128]{3,1,2,0:T(4,128)}, u32[]{:S(2)}) copy-start(s32[1,4,4,128]{3,1,2,0:T(4,128)} %copy-done.9) | copy-start | bytes 24580
  110.1 7.6 %copy-start.12 = (bf16[1,4,4,128]{3,1,2,0:T(4,128)(2,1)S(1)}, bf16[1,4,4,128]{3,1,2,0:T(4,128)(2,1)}, u32[]{:S(2)}) copy-start(bf16[1,4,4,128]{3,1,2,0:T(4,128)(2,1)} %copy-done.11) | copy-start | bytes 12292
  110.2 7.6 %copy-start.14 = (bf16[4,128]{1,0:T(4,128)(2,1)S(1)}, bf16[4,128]{1,0:T(4,128)(2,1)}, u32[]{:S(2)}) copy-start(bf16[4,128]{1,0:T(4,128)(2,1)} %copy-done.13) | copy-start | bytes 3076
  110.2 7.6 %copy-start.16 = (f32[1,2048,1]{1,2,0:T(1,128)S(1)}, f32[1,2048,1]{1,2,0:T(1,128)}, u32[]{:S(2)}) copy-start(f32[1,2048,1]{1,2,0:T(1,128)} %copy-done.15) | copy-start | bytes 24580
  115.4 13.5 %collective-permute-start.7 = (bf16[2,512,128]{2,1,0:T(8,128)(2,1)}, bf16[2,512,128]{2,1,0:T(8,128)(2,1)}, u32[]{:S(2)}, u32[]{:S(2)}) collective-permute-start(bf16[2,512,128]{2,1,0:T(8,128)(2,1)} %add_convert_fusion.1), channel_id=1, source_target_pairs={{4,0},{8,4},{12,8},{16,12},{20,16},{24,20},{28,24},{32,28},{36,32}... | collective-permute-start | bytes 786440 | tf_op jit(solution)/shard_map/ppermute | solution.py:17
  121.1 14.4 %all-to-all-start.6 = ((bf16[4,128,512]{2,1,0:T(8,128)(2,1)}), bf16[4,128,512]{2,1,0:T(8,128)(2,1)S(1)}, u32[]{:S(2)}, u32[]{:S(2)}) async-start(bf16[4,128,512]{2,1,0:T(8,128)(2,1)} %convert_element_type.122), calls=%async_computation.6 | async-start | bytes 1048576 | tf_op jit(solution)/shard_map/all_to_all | solution.py:155
  135.5 10.1 %all-to-all-start.7 = ((bf16[2,512,128]{2,0,1:T(2,128)(2,1)}), bf16[2,512,128]{2,0,1:T(2,128)(2,1)S(1)}, u32[]{:S(2)}, u32[]{:S(2)}) async-start(bf16[2,512,128]{2,0,1:T(2,128)(2,1)} %copy.53), calls=%async_computation.7 | async-start | bytes 524288 | tf_op jit(solution)/shard_map/all_to_all | solution.py:149
  (1 other events, 0.8 us)
where the time goes:
time: 148 us; the launch traced here: 147 us
  starting transfers between devices  55.1 us (37%)
  matrix products  31.3 us (21%)
  waiting for transfers between devices  29.7 us (20%)
  local copies, waits for them, and re-layouts  17.8 us (12%)
  other arithmetic  12.1 us (8%)
    ppermute x8, starting transfers between devices, passed_along(): return lax.ppermute(block, axis, route)  23.4 us
    dot_general x5, matrix products, block_scores(): jnp.einsum('grd,gkd->grk', rows_query, key_part_blk, preferred_element_ty...  9.49 us
    dot_general x3, matrix products, backward_tile(): jnp.einsum('grk,gkd->grd', dscore, block[0], preferred_element_type=jnp.f...  6.98 us
    all_to_all x1, waiting for transfers between devices, on_device(): lax.all_to_all(values, 'uly', split_axis=1, concat_axis=0, tiled=True)  5.93 us
    dot_general x3, matrix products, backward_tile(): jnp.einsum('grd,gkd->grk', rows_grad, block[1], preferred_element_type=jn...  5.26 us
    all_to_all x1, waiting for transfers between devices, on_device(): lax.all_to_all(carried.astype(jnp.bfloat16), 'uly', split_axis=1, concat_...  4.86 us
    all_to_all x1, starting transfers between devices, on_device(): lax.all_to_all(out_grad, 'uly', split_axis=1, concat_axis=0, tiled=True)  4.75 us
    all_to_all x1, starting transfers between devices, on_device(): lax.all_to_all(query_cols.astype(jnp.bfloat16), 'uly', split_axis=0, conc...  4.74 us
  transfers between devices with their start and end apart: 16, of which 9 were waited for; matrix products, arithmetic and copies ran while one was open for 35% of the time, Pallas kernels for 0%

commit v1 on v0

v1 whole, which is shorter than its diff:
```python
import math

import jax
import jax.numpy as jnp
from jax import lax
from jax.experimental import pallas as pl
from jax.experimental.pallas import tpu as pltpu
from jax.sharding import PartitionSpec as P

HD = 128
KVH = 4
QH = 16
PAIRS = 8
TOK = 128
TILES = 9
C2 = HD ** -0.5 * math.log2(math.e)
SCALE = HD ** -0.5
LOW = -1e30
NT = (((1,), (1,)), ((), ()))
F32 = jnp.float32
BF16 = jnp.bfloat16


def kernel(q_hbm, k_hbm, v_hbm, g_hbm, docs_ref, o_hbm, dq_hbm, dk_hbm, dv_hbm,
           kv, dd, qs, gs, gt, s_ref, dp_ref, ot, dqt, m_ref, l_ref, dl_ref,
           ct, rx, o_buf, dq_buf, dk_buf, dv_buf,
           lsem, osem, gsend, grecv, rsend, rrecv):
    x = lax.axis_index("uly")
    blk = lax.axis_index("blk")
    blks = lax.axis_size("blk")
    core = lax.rem(blk, 2)
    xr, x2, xl = lax.rem(x + 1, 4), lax.rem(x + 2, 4), lax.rem(x + 3, 4)
    right, left = {"uly": xr}, {"uly": xl}
    ahead = {"blk": lax.rem(blk + 2, blks)}
    behind = {"blk": lax.rem(blk + blks - 2, blks)}
    sibling = {"blk": blk + 1 - 2 * core}

    loads = [
        pltpu.make_async_copy(k_hbm, kv.at[8 + x, 0], lsem.at[0]),
        pltpu.make_async_copy(v_hbm, kv.at[8 + x, 1], lsem.at[1]),
    ]
    for h in range(QH):
        cols = pl.ds(h * HD, HD)
        loads.append(pltpu.make_async_copy(q_hbm.at[:, cols], qs.at[h], lsem.at[2 + h]))
    for h in range(QH):
        cols = pl.ds(h * HD, HD)
        loads.append(pltpu.make_async_copy(g_hbm.at[:, cols], gs.at[h], lsem.at[2 + QH + h]))
    for load in loads:
        load.start()

    barrier = pltpu.get_barrier_semaphore()
    for dev in (right, left, ahead, behind, sibling):
        pl.semaphore_signal(barrier, inc=1, device_id=dev, device_id_type=pl.DeviceIdType.MESH)
    dd[8 + x] = jnp.broadcast_to(docs_ref[...], (8, TOK))
    loads[0].wait()
    loads[1].wait()
    pl.semaphore_wait(barrier, 5)

    def view(slot, part):
        return dd.at[slot] if part == 2 else kv.at[slot, part]

    def gather_copy(n, src, dst, part, dev):
        return pltpu.make_async_remote_copy(
            src_ref=view(src, part), dst_ref=view(dst, part),
            send_sem=gsend.at[n, part], recv_sem=grecv.at[dst, part],
            device_id=dev, device_id_type=pl.DeviceIdType.MESH)

    def send(n, src, dst, parts, dev):
        for part in parts:
            gather_copy(n, src, dst, part, dev).start()

    def arrived(slot, parts):
        for part in parts:
            gather_copy(0, slot, slot, part, right).wait_recv()

    ALL = (2, 0, 1)
    send(0, 8 + x, 8 + x, (2, 0, 1), right)
    send(1, 8 + x, 8 + x, (2, 1, 0), left)
    send(2, 8 + x, x, ALL, ahead)

    @pl.when(core == 0)
    def _():
        send(3, 8 + x, 4 + x, ALL, sibling)

    for slot in (0, 1, 2, 9, 10, 11):
        ct[slot] = jnp.zeros((2, TOK, KVH * HD), BF16)
    m_ref[...] = jnp.full(m_ref.shape, LOW, F32)
    l_ref[...] = jnp.zeros(l_ref.shape, F32)
    ot[...] = jnp.zeros(ot.shape, F32)
    dqt[...] = jnp.zeros(dqt.shape, F32)
    for load in loads[2:]:
        load.wait()
    for u in range(PAIRS):
        for i in range(2):
            gt[u, :, i * TOK:(i + 1) * TOK] = gs[2 * u + i].astype(F32).T
    docs_row = docs_ref[...]

    def cross(k):
        return x + k + 4 * ((x + k) // 4)

    def pick(order, index):
        slot = order[0]
        for i in range(1, TILES):
            slot = jnp.where(index == i, order[i], slot)
        return slot

    def on_own_neighbours():
        arrived(8 + xl, ALL)
        send(4, 8 + xl, 8 + xl, (2, 0), right)
        arrived(8 + xr, ALL)
        send(5, 8 + xr, 8 + xr, (1,), left)

        @pl.when(core == 0)
        def _():
            send(6, 8 + xl, 4 + xl, ALL, sibling)
            send(7, 8 + xr, 4 + xr, ALL, sibling)

    def on_earlier():
        arrived(x, ALL)
        send(8, x, x, ALL, right)
        send(9, x, x, ALL, left)

        @pl.when(core == 1)
        def _():
            send(3, x, 4 + x, ALL, sibling)

    def on_own_far():
        arrived(8 + x2, ALL)
        send(10, 8 + x2, x2, ALL, ahead)

        @pl.when(core == 0)
        def _():
            send(11, 8 + x2, 4 + x2, ALL, sibling)

    def on_earlier_neighbours():
        for slot in (xl, xr):
            arrived(slot, ALL)

        @pl.when(core == 1)
        def _():
            send(6, xl, 4 + xl, ALL, sibling)
            send(7, xr, 4 + xr, ALL, sibling)

    def on_earlier_far():
        arrived(x2, ALL)

        @pl.when(core == 1)
        def _():
            send(11, x2, 4 + x2, ALL, sibling)

    fwd_order = (8 + x, x, 4 + x, 4 + xr, 4 + xl, cross(1), cross(3), 4 + x2, cross(2))

    def forward(index, carry):
        slot = pick(fwd_order, index)

        @pl.when(index == 1)
        def _():
            on_own_neighbours()
            on_earlier()

        @pl.when(index == 2)
        def _():
            arrived(4 + x, ALL)

        @pl.when(index == 3)
        def _():
            on_own_far()
            on_earlier_neighbours()
            arrived(4 + xr, ALL)
            arrived(4 + xl, ALL)

        @pl.when(index == 7)
        def _():
            on_earlier_far()
            arrived(4 + x2, ALL)

        place = slot - x
        key_docs = jnp.broadcast_to(dd[slot][0:1], (TOK, TOK)).T
        key_at = lax.broadcasted_iota(jnp.int32, (TOK, TOK), 0) + (place - 8) * TOK
        row_at = lax.broadcasted_iota(jnp.int32, (TOK, TOK), 1)
        allowed = (key_docs == docs_row) & (key_at <= row_at)
        bias = jnp.where(allowed, 0.0, LOW).astype(F32)
        bias = jnp.concatenate([bias, bias], axis=1)
        for u in range(PAIRS):
            cols = slice((u // 2) * HD, (u // 2 + 1) * HD)
            key, value = kv[slot, 0, :, cols], kv[slot, 1, :, cols]
            query = qs[2 * u:2 * u + 2].reshape(2 * TOK, HD)
            grad = gs[2 * u:2 * u + 2].reshape(2 * TOK, HD)
            scores = lax.dot_general(key, query, NT, preferred_element_type=F32) * C2 + bias
            s_ref[place, u] = scores
            dp_ref[place, u] = lax.dot_general(value, grad, NT, preferred_element_type=F32)
            top = m_ref[u]
            new_top = jnp.maximum(top, jnp.max(scores, axis=0, keepdims=True))
            factor = jnp.exp2(top - new_top)
            weights = jnp.exp2(scores - new_top)
            m_ref[u] = new_top
            l_ref[u] = l_ref[u] * factor + jnp.sum(weights, axis=0, keepdims=True)
            ot[u] = ot[u] * factor + jnp.dot(
                value.T, weights.astype(BF16), preferred_element_type=F32)
        return carry

    lax.fori_loop(0, TILES, forward, 0)

    for u in range(PAIRS):
        total = l_ref[u]
        out = (ot[u] / total).astype(BF16).astype(F32)
        ot[u] = out
        dl_ref[u] = jnp.sum(out * gt[u], axis=0, keepdims=True)
        m_ref[u] = m_ref[u] + jnp.log2(total)

    def reduce_copy(n, src, dst, part, dev):
        return pltpu.make_async_remote_copy(
            src_ref=ct.at[src, part], dst_ref=rx.at[dst, part],
            send_sem=rsend.at[n, part], recv_sem=rrecv.at[dst, part],
            device_id=dev, device_id_type=pl.DeviceIdType.MESH)

    def give(n, src, dst, parts, dev):
        for part in parts:
            reduce_copy(n, src, dst, part, dev).start()

    def add(slot, dst, parts):
        for part in parts:
            reduce_copy(0, slot, dst, part, right).wait_recv()
            ct[slot, part] = (ct[slot, part].astype(F32) + rx[dst, part].astype(F32)).astype(BF16)

    base = 8 - 8 * core
    BOTH = (0, 1)
    bwd_order = (4 + x2, cross(2), 4 + xr, 4 + xl, cross(1), cross(3), 4 + x, x, 8 + x)

    def backward(index, carry):
        slot = pick(bwd_order, index)
        place = slot - x
        for g in range(KVH):
            cols = slice(g * HD, (g + 1) * HD)
            key = kv[slot, 0, :, cols]
            key_t = key.T
            key_grad = jnp.zeros((TOK, HD), F32)
            value_grad = jnp.zeros((TOK, HD), F32)
            for u in (2 * g, 2 * g + 1):
                query = qs[2 * u:2 * u + 2].reshape(2 * TOK, HD)
                grad = gs[2 * u:2 * u + 2].reshape(2 * TOK, HD)
                probs = jnp.exp2(s_ref[place, u] - m_ref[u])
                dscore = (probs * (dp_ref[place, u] - dl_ref[u])).astype(BF16)
                value_grad += jnp.dot(probs.astype(BF16), grad, preferred_element_type=F32)
                key_grad += jnp.dot(dscore, query, preferred_element_type=F32)
                dqt[u] += jnp.dot(key_t, dscore, preferred_element_type=F32)
            ct[slot, 0, :, cols] = key_grad.astype(BF16)
            ct[slot, 1, :, cols] = value_grad.astype(BF16)

        @pl.when(index == 0)
        def _():
            give(0, 4 + x2, x2, BOTH, sibling)

        @pl.when(index == 1)
        def _():
            add(base + x2, x2, BOTH)
            give(1, x2, 4, BOTH, behind)

        @pl.when(index == 2)
        def _():
            give(2, 4 + xr, xr, BOTH, sibling)

        @pl.when(index == 3)
        def _():
            give(3, 4 + xl, xl, BOTH, sibling)

        @pl.when(index == 5)
        def _():
            add(base + xr, xr, BOTH)
            add(base + xl, xl, BOTH)
            give(4, xr, 8, BOTH, right)
            give(5, xl, 9, BOTH, left)
            give(6, 8 + xr, 6, (1,), right)
            give(7, 8 + xl, 7, (0,), left)

        @pl.when(index == 6)
        def _():
            give(8, 4 + x, x, BOTH, sibling)

        return carry

    lax.fori_loop(0, TILES, backward, 0)

    add(base + x, x, BOTH)
    add(8 + x2, 4, BOTH)
    give(9, 8 + x2, 5, (0,), right)
    give(10, 8 + x2, 5, (1,), left)

    for u in range(PAIRS):
        for i in range(2):
            h = 2 * u + i
            cols, rows = slice(h * HD, (h + 1) * HD), slice(i * TOK, (i + 1) * TOK)
            o_buf[:, cols] = ot[u, :, rows].T.astype(BF16)
            dq_buf[:, cols] = dqt[u, :, rows].T * SCALE
    outs = [
        pltpu.make_async_copy(o_buf, o_hbm, osem.at[0]),
        pltpu.make_async_copy(dq_buf, dq_hbm, osem.at[1]),
        pltpu.make_async_copy(dk_buf, dk_hbm, osem.at[2]),
        pltpu.make_async_copy(dv_buf, dv_hbm, osem.at[3]),
    ]
    outs[0].start()
    outs[1].start()

    add(x, 8, BOTH)
    add(x, 9, BOTH)
    give(11, x, 10, BOTH, behind)
    add(8 + xr, 5, (0,))
    give(6, 8 + xr, 6, (0,), right)
    add(8 + xl, 5, (1,))
    give(7, 8 + xl, 7, (1,), left)

    for part, buf in ((0, dk_buf), (1, dv_buf)):
        total = ct[8 + x, part].astype(F32)
        for dst in (6, 7, 10):
            reduce_copy(0, x, dst, part, right).wait_recv()
            total = total + rx[dst, part].astype(F32)
        buf[...] = total * SCALE if part == 0 else total
        outs[2 + part].start()

    for n in range(12):
        for part in (2, 0, 1):
            if (n, part) in ((4, 1), (5, 0), (5, 2)):
                continue
            gather_copy(n, x, x, part, right).wait_send()
    for n in range(12):
        for part in BOTH:
            if (n, part) in ((9, 1), (10, 0)):
                continue
            reduce_copy(n, x, x, part, right).wait_send()
    for out in outs:
        out.wait()


def on_device(queries, keys, values, out_grad, docs):
    rows, width, kv_width = TOK, QH * HD, KVH * HD
    any_spec = pl.BlockSpec(memory_space=pl.ANY)
    vmem_spec = pl.BlockSpec(memory_space=pltpu.VMEM)
    return pl.pallas_call(
        kernel,
        out_shape=(
            jax.ShapeDtypeStruct((rows, width), BF16),
            jax.ShapeDtypeStruct((rows, width), F32),
            jax.ShapeDtypeStruct((rows, kv_width), F32),
            jax.ShapeDtypeStruct((rows, kv_width), F32),
        ),
        in_specs=[any_spec] * 4 + [vmem_spec],
        out_specs=(any_spec,) * 4,
        scratch_shapes=[
            pltpu.VMEM((12, 2, TOK, kv_width), BF16),
            pltpu.VMEM((12, 8, TOK), jnp.int32),
            pltpu.VMEM((QH, TOK, HD), BF16),
            pltpu.VMEM((QH, TOK, HD), BF16),
            pltpu.VMEM((PAIRS, HD, 2 * TOK), F32),
            pltpu.VMEM((TILES, PAIRS, TOK, 2 * TOK), F32),
            pltpu.VMEM((TILES, PAIRS, TOK, 2 * TOK), F32),
            pltpu.VMEM((PAIRS, HD, 2 * TOK), F32),
            pltpu.VMEM((PAIRS, HD, 2 * TOK), F32),
            pltpu.VMEM((PAIRS, 1, 2 * TOK), F32),
            pltpu.VMEM((PAIRS, 1, 2 * TOK), F32),
            pltpu.VMEM((PAIRS, 1, 2 * TOK), F32),
            pltpu.VMEM((12, 2, TOK, kv_width), BF16),
            pltpu.VMEM((11, 2, TOK, kv_width), BF16),
            pltpu.VMEM((rows, width), BF16),
            pltpu.VMEM((rows, width), F32),
            pltpu.VMEM((rows, kv_width), F32),
            pltpu.VMEM((rows, kv_width), F32),
            pltpu.SemaphoreType.DMA((2 + 2 * QH,)),
            pltpu.SemaphoreType.DMA((4,)),
            pltpu.SemaphoreType.DMA((12, 3)),
            pltpu.SemaphoreType.DMA((12, 3)),
            pltpu.SemaphoreType.DMA((12, 2)),
            pltpu.SemaphoreType.DMA((11, 2)),
        ],
        compiler_params=pltpu.CompilerParams(
            collective_id=0, has_side_effects=True, vmem_limit_bytes=56 * 1024 * 1024),
    )(queries, keys, values, out_grad, docs.reshape(1, TOK))


def solution(mesh):
    spec = P(("blk", "uly"), None)
    return jax.shard_map(
        on_device,
        mesh=mesh,
        in_specs=(spec, spec, spec, spec, P(("blk", "uly"))),
        out_specs=(spec, spec, spec, spec),
        check_vma=False,
    )
```

time: 148 us -> 70.9 us (0.48)
  the two profiles are of different devices: /device:TPU:384 before, /device:TPU:2 now
where the time goes in v1:
time: 70.9 us; the launch traced here: 70.7 us
  Pallas kernels  65.2 us (92%)
  local copies, waits for them, and re-layouts  4.81 us (7%)
    pallas_call x1, Pallas kernels, on_device(): pl.pallas_call(kernel, out_shape=(jax.ShapeDtypeStruct((rows, width), BF1...  65.2 us
    unnamed x10, local copies, waits for them, and re-layouts  4.81 us

profile of v1, /device:TPU:2, one launch (start us, length us, event | category | flops | bytes accessed | tf_op | source)
XLA Modules:
  0.0 70.7 jit_solution(3196420618279155440)
XLA Ops:
  0.6 65.2 %shard_map.84 = (bf16[128,2048]{1,0:T(8,128)(2,1)}, f32[128,2048]{1,0:T(8,128)}, f32[128,512]{1,0:T(8,128)}, f32[128,512]{1,0:T(8,128)}) custom-call(bf16[128,2048]{1,0:T(8,128)(2,1)} %q_hbm.1, bf16[128,512]{1,0:T(8,128)(2,1)} %k_hbm.1, bf16[128,512]{1,0:T(8,128)(2,1)} %v_hbm.1, bf16[128,2048]{1,0:T(8,128)(2,1)} %g_hbm.1, s32[1,128]{1,0:T(1,128)} %bitcast.1), custom_call_target="tpu_custom_call" | custom-call | tf_op jit(solution)/shard_map/pallas_call | solution.py:338
  65.8 0.0 copy-start
  65.8 2.0 %copy.13 = bf16[128,2048]{1,0:T(8,128)(2,1)} copy(bf16[128,2048]{1,0:T(8,128)(2,1)} %get-tuple-element.8) | data formatting | bytes 1048576
  67.8 0.0 copy-done
  67.8 0.0 copy-start.2
  67.8 1.0 %copy.14 = f32[128,2048]{1,0:T(8,128)} copy(f32[128,2048]{1,0:T(8,128)S(1)} %copy-done) | data formatting | bytes 2097152
  68.8 0.1 copy-done.2
  68.9 0.0 copy-start.1
  68.9 0.7 copy.15
  69.6 0.3 copy-done.1
  70.0 0.7 copy.16
Async XLA Ops:
  65.8 2.0 %copy-start = (f32[128,2048]{1,0:T(8,128)S(1)}, f32[128,2048]{1,0:T(8,128)}, u32[]{:S(2)}) copy-start(f32[128,2048]{1,0:T(8,128)} %get-tuple-element.9) | copy-start | bytes 3145732
  67.8 1.1 %copy-start.2 = (f32[128,512]{1,0:T(8,128)S(1)}, f32[128,512]{1,0:T(8,128)}, u32[]{:S(2)}) copy-start(f32[128,512]{1,0:T(8,128)} %get-tuple-element.10) | copy-start | bytes 786436
  68.9 1.0 %copy-start.1 = (f32[128,512]{1,0:T(8,128)S(1)}, f32[128,512]{1,0:T(8,128)}, u32[]{:S(2)}) copy-start(f32[128,512]{1,0:T(8,128)} %get-tuple-element.11) | copy-start | bytes 786436

commit v2 on v0

v2 whole, which is shorter than its diff:
```python
import math

import jax
import jax.numpy as jnp
from jax import lax
from jax.experimental import pallas as pl
from jax.experimental.pallas import tpu as pltpu
from jax.sharding import PartitionSpec as P

HD = 128
KVH = 4
QH = 16
GQ = 4
TOK = 128
LANES = 4
TILES = 9
C2 = HD ** -0.5 * math.log2(math.e)
SCALE = HD ** -0.5
LOW = -1e30
NT = (((1,), (1,)), ((), ()))
F32 = jnp.float32
BF16 = jnp.bfloat16
MESH = pl.DeviceIdType.MESH
WIDE = GQ * HD


def kernel(q_hbm, k_hbm, v_hbm, g_hbm, docs_ref, o_out, dq_out, dkv_out,
           kv, kt, vt, dd, kd, qs, gs, s_ref, ot, dqt, m_ref, l_ref, dl_ref,
           da, ct, fin, rxs, rxy, o_buf, dq_buf,
           lsem, osem, asend, arecv, bsend, brecv, ssend, srecv, dsem, drecv,
           rssend, rsrecv, rysend, ryrecv, osend, orecv):
    x = lax.axis_index("uly")
    blk = lax.axis_index("blk")
    blks = lax.axis_size("blk")
    core = lax.rem(blk, 2)
    peers = tuple(lax.rem(x + k, 4) for k in (2, 1, 3))
    ahead, behind = {"blk": blk + 2}, {"blk": blk - 2}
    sibling = {"blk": blk + 1 - 2 * core}
    when_ahead, when_behind = pl.when(blk < blks - 2), pl.when(blk >= 2)
    when_before = pl.when(blk >= 1)
    when_core0, when_core1 = pl.when(core == 0), pl.when(core == 1)

    def cols(index, width):
        return pl.ds(pl.multiple_of(index * width, width), width)

    def remote(src, dst, send_sem, recv_sem, dev):
        return pltpu.make_async_remote_copy(
            src_ref=src, dst_ref=dst, send_sem=send_sem, recv_sem=recv_sem,
            device_id=dev, device_id_type=MESH)

    def exchange(part, n):
        peer = peers[n]
        src, dst = (
            (k_hbm.at[:, cols(peer, HD)], kv.at[8 + x, 0]),
            (v_hbm.at[:, cols(peer, HD)], kv.at[8 + x, 1]),
            (dd.at[8 + x], dd.at[8 + x]),
            (q_hbm.at[:, cols(peer, WIDE)], qs.at[x]),
            (g_hbm.at[:, cols(peer, WIDE)], gs.at[x]),
        )[part]
        return remote(src, dst, asend.at[part, n], arecv.at[part, x], {"uly": peer})

    def exchanged(part, n):
        origin = peers[n]
        dst = (kv.at[8 + origin, 0], kv.at[8 + origin, 1], dd.at[8 + origin],
               qs.at[origin], gs.at[origin])[part]
        remote(dst, dst, asend.at[part, n], arecv.at[part, origin], {"uly": origin}).wait_recv()

    loads = [
        pltpu.make_async_copy(k_hbm.at[:, cols(x, HD)], kv.at[8 + x, 0], lsem.at[0]),
        pltpu.make_async_copy(v_hbm.at[:, cols(x, HD)], kv.at[8 + x, 1], lsem.at[1]),
        pltpu.make_async_copy(q_hbm.at[:, cols(x, WIDE)], qs.at[x], lsem.at[2]),
        pltpu.make_async_copy(g_hbm.at[:, cols(x, WIDE)], gs.at[x], lsem.at[3]),
    ]
    for load in loads:
        load.start()

    barrier = pltpu.get_barrier_semaphore()

    def greet(dev):
        pl.semaphore_signal(barrier, inc=1, device_id=dev, device_id_type=MESH)

    for peer in peers:
        greet({"uly": peer})
    greet(sibling)
    when_ahead(lambda: greet(ahead))
    when_behind(lambda: greet(behind))
    dd[8 + x] = jnp.broadcast_to(docs_ref[...], (8, TOK))
    pl.semaphore_wait(barrier, 4 + jnp.where(blk < blks - 2, 1, 0) + jnp.where(blk >= 2, 1, 0))

    for part in (0, 1, 2, 3):
        for n in range(3):
            exchange(part, n).start()

    def forward_block(k):
        return remote(kv.at[8 + k], kv.at[k], bsend.at[k], brecv.at[k], ahead)

    def forward_docs():
        return remote(dd.at[8:12], dd.at[0:4], dsem.at[0], drecv.at[0], ahead)

    def sibling_blocks(row):
        return remote(kv.at[pl.ds(row, 4)], kv.at[4:8], ssend.at[0], srecv.at[0], sibling)

    def sibling_docs(row):
        return remote(dd.at[pl.ds(row, 4)], dd.at[4:8], ssend.at[1], srecv.at[1], sibling)

    loads[0].wait()
    loads[1].wait()
    when_ahead(lambda: forward_block(x).start())

    def absent(row):
        kv[row:row + 4] = jnp.zeros((4, 2, TOK, HD), BF16)
        dd[row:row + 4] = jnp.full((4, 8, TOK), -1, jnp.int32)

    pl.when(blk < 2)(lambda: absent(0))
    pl.when(blk < 1)(lambda: absent(4))

    m_ref[...] = jnp.full(m_ref.shape, LOW, F32)
    l_ref[...] = jnp.zeros(l_ref.shape, F32)
    ot[...] = jnp.zeros(ot.shape, F32)
    dqt[...] = jnp.zeros(dqt.shape, F32)
    da[...] = jnp.zeros(da.shape, F32)

    for n in (1, 2, 0):
        for part in (0, 1, 2):
            exchanged(part, n)
        when_ahead(lambda: forward_block(peers[n]).start())
    when_ahead(lambda: forward_docs().start())

    @when_core0
    def _():
        sibling_blocks(8).start()
        sibling_docs(8).start()

    for n in range(3):
        exchange(4, n).start()

    def prepare(row):
        for t in range(row, row + 4):
            kt[t] = kv[t, 0].T
            vt[t] = kv[t, 1].T
            kd[t] = jnp.broadcast_to(dd[t][0:1], (TOK, TOK)).T

    prepare(8)
    loads[2].wait()
    for n in range(3):
        exchanged(3, n)

    def two_back():
        @when_behind
        def _():
            for k in range(4):
                remote(kv.at[k], kv.at[k], bsend.at[k], brecv.at[k], behind).wait_recv()
            forward_docs().wait_recv()

            @when_core1
            def _():
                sibling_blocks(0).start()
                sibling_docs(0).start()

        prepare(0)

    def one_back():
        @when_before
        def _():
            sibling_blocks(0).wait_recv()
            sibling_docs(0).wait_recv()

        prepare(4)

    def heads(ref, i, p):
        lo = 2 * p * HD
        return jnp.concatenate([ref[i, :, lo:lo + HD], ref[i, :, lo + HD:lo + 2 * HD]], axis=0)

    def tile(one_row, k, i):
        return jnp.where(one_row, 4 + k, jnp.where(i <= k, k, 9 + k))

    def forward(index, carry):
        @pl.when((index == 1) & (core == 0) | (index == 5) & (core == 1))
        def _():
            two_back()

        @pl.when((index == 1) & (core == 1) | (index == 5) & (core == 0))
        def _():
            one_back()

        phase = (index + 3) // 4
        k = index - 1 - 4 * (phase - 1)
        k = jnp.where(index == 0, -1, k)
        one_row = (index > 0) & (lax.rem(phase + core, 2) == 0)
        for i in range(LANES):
            t = tile(one_row, k, i)
            key_at = lax.broadcasted_iota(jnp.int32, (TOK, TOK), 0) + (t - 8 - i) * TOK
            row_at = lax.broadcasted_iota(jnp.int32, (TOK, TOK), 1)
            allowed = (kd[t] == dd[8 + i][0:1]) & (key_at <= row_at)
            bias = jnp.where(allowed, 0.0, LOW).astype(F32)
            bias = jnp.concatenate([bias, bias], axis=1)
            for p in range(2):
                scores = lax.dot_general(
                    kv[t, 0], heads(qs, i, p), NT, preferred_element_type=F32) * C2 + bias
                s_ref[i, t - i, p] = scores
                top = m_ref[i, p]
                new_top = jnp.maximum(top, jnp.max(scores, axis=0, keepdims=True))
                factor = jnp.exp2(top - new_top)
                weights = jnp.exp2(scores - new_top)
                m_ref[i, p] = new_top
                l_ref[i, p] = l_ref[i, p] * factor + jnp.sum(weights, axis=0, keepdims=True)
                ot[i, p] = ot[i, p] * factor + jnp.dot(
                    vt[t], weights.astype(BF16), preferred_element_type=F32)
        return carry

    lax.fori_loop(0, TILES, forward, 0)

    loads[3].wait()
    for n in range(3):
        exchanged(4, n)

    for i in range(LANES):
        for p in range(2):
            total = l_ref[i, p]
            out = (ot[i, p] / total).astype(BF16)
            m_ref[i, p] = m_ref[i, p] + jnp.log2(total)
            for e in range(2):
                lo = (2 * p + e) * HD
                half = out[:, e * TOK:(e + 1) * TOK]
                o_buf[i, :, lo:lo + HD] = half.T
                grad_t = gs[i, :, lo:lo + HD].T.astype(F32)
                dl_ref[i, p, :, e * TOK:(e + 1) * TOK] = jnp.sum(
                    grad_t * half.astype(F32), axis=0, keepdims=True)

    def deliver(kind, n):
        peer = peers[n]
        src, dst = ((o_buf.at[peer], o_out.at[x]), (dq_buf.at[peer], dq_out.at[x]),
                    (fin.at[peer], dkv_out.at[x]))[kind]
        return remote(src, dst, osend.at[kind, n], orecv.at[kind, x], {"uly": peer})

    def delivered(kind, n):
        origin = peers[n]
        dst = (o_out, dq_out, dkv_out)[kind].at[origin]
        remote(dst, dst, osend.at[kind, n], orecv.at[kind, origin], {"uly": origin}).wait_recv()

    keep = [
        pltpu.make_async_copy(o_buf.at[x], o_out.at[x], osem.at[0]),
        pltpu.make_async_copy(dq_buf.at[x], dq_out.at[x], osem.at[1]),
        pltpu.make_async_copy(fin.at[x], dkv_out.at[x], osem.at[2]),
    ]
    keep[0].start()
    for n in range(3):
        deliver(0, n).start()

    def to_sibling(k):
        return remote(ct.at[4 + k], rxs.at[k], rssend.at[k], rsrecv.at[k], sibling)

    def to_behind(k):
        return remote(ct.at[k], rxy.at[k], rysend.at[k], ryrecv.at[k], behind)

    def step(n):
        off = jnp.where(n == 0, 2, jnp.where(n == 1, 1, jnp.where(n == 2, 3, 0)))
        return lax.rem(x + off, 4)

    def backward(index, carry):
        phase = index // 4
        k = jnp.where(index == 8, -1, step(index - 4 * phase))
        one_row = (index < 8) & (lax.rem(phase + core, 2) == 0)
        for i in range(LANES):
            t = tile(one_row, k, i)
            key_grad = jnp.zeros((TOK, HD), F32)
            value_grad = jnp.zeros((TOK, HD), F32)
            for p in range(2):
                query, grad = heads(qs, i, p), heads(gs, i, p)
                probs = jnp.exp2(s_ref[i, t - i, p] - m_ref[i, p])
                dprob = lax.dot_general(kv[t, 1], grad, NT, preferred_element_type=F32)
                dscore = (probs * (dprob - dl_ref[i, p])).astype(BF16)
                value_grad += jnp.dot(probs.astype(BF16), grad, preferred_element_type=F32)
                key_grad += jnp.dot(dscore, query, preferred_element_type=F32)
                dqt[i, p] += jnp.dot(kt[t], dscore, preferred_element_type=F32)
            da[t, 0] += key_grad
            da[t, 1] += value_grad

        @pl.when(one_row)
        def _():
            ct[4 + k] = da[4 + k].astype(BF16)
            when_before(lambda: to_sibling(k).start())

        @pl.when((core == 0) & (phase == 1))
        def _():
            ct[k] = da[k].astype(BF16)
            when_behind(lambda: to_behind(k).start())

        @pl.when((core == 1) & (index >= 2) & (index < 6) & (blk >= 2))
        def _():
            j = step(index - 2)
            to_sibling(j).wait_recv()
            ct[j] = (da[j] + rxs[j].astype(F32)).astype(BF16)
            to_behind(j).start()

        return carry

    lax.fori_loop(0, TILES, backward, 0)

    for i in range(LANES):
        for p in range(2):
            for e in range(2):
                lo = (2 * p + e) * HD
                dq_buf[i, :, lo:lo + HD] = (
                    dqt[i, p, :, e * TOK:(e + 1) * TOK].T * SCALE).astype(BF16)
    keep[1].start()
    for n in range(3):
        deliver(1, n).start()

    @when_core0
    def _():
        for k in range(4):
            to_sibling(k).wait_recv()
            da[8 + k] += rxs[k].astype(F32)

    for n in range(4):
        k = (peers + (x,))[n]

        @when_ahead
        def _():
            to_behind(k).wait_recv()
            da[8 + k] += rxy[k].astype(F32)

        fin[k] = da[8 + k].astype(BF16)
        if n < 3:
            deliver(2, n).start()
    keep[2].start()

    for part in range(5):
        for n in range(3):
            exchange(part, n).wait_send()
    for kind in range(3):
        for n in range(3):
            delivered(kind, n)
            deliver(kind, n).wait_send()
        keep[kind].wait()

    @when_ahead
    def _():
        for k in range(4):
            forward_block(k).wait_send()
        forward_docs().wait_send()

    @pl.when(blk != 1)
    def _():
        sibling_blocks(0).wait_send()
        sibling_docs(0).wait_send()

    @when_before
    def _():
        for k in range(4):
            to_sibling(k).wait_send()

    @when_behind
    def _():
        for k in range(4):
            to_behind(k).wait_send()


def finish(o_ref, dq_ref, dkv_ref, o_out, dq_out, dk_out, dv_out):
    o_out[...] = o_ref[0]
    dq_out[...] = dq_ref[0].astype(F32)
    dk_out[...] = dkv_ref[0, 0].astype(F32) * SCALE
    dv_out[...] = dkv_ref[0, 1].astype(F32)


def on_device(queries, keys, values, out_grad, docs):
    any_spec = pl.BlockSpec(memory_space=pl.ANY)
    vmem_spec = pl.BlockSpec(memory_space=pltpu.VMEM)
    dma = pltpu.SemaphoreType.DMA
    stat = pltpu.VMEM((LANES, 2, 1, 2 * TOK), F32)
    parts = pl.pallas_call(
        kernel,
        out_shape=(
            jax.ShapeDtypeStruct((LANES, TOK, WIDE), BF16),
            jax.ShapeDtypeStruct((LANES, TOK, WIDE), BF16),
            jax.ShapeDtypeStruct((LANES, 2, TOK, HD), BF16),
        ),
        in_specs=[any_spec] * 4 + [vmem_spec],
        out_specs=(any_spec,) * 3,
        scratch_shapes=[
            pltpu.VMEM((12, 2, TOK, HD), BF16),
            pltpu.VMEM((12, HD, TOK), BF16),
            pltpu.VMEM((12, HD, TOK), BF16),
            pltpu.VMEM((12, 8, TOK), jnp.int32),
            pltpu.VMEM((12, TOK, TOK), jnp.int32),
            pltpu.VMEM((LANES, TOK, WIDE), BF16),
            pltpu.VMEM((LANES, TOK, WIDE), BF16),
            pltpu.VMEM((LANES, TILES, 2, TOK, 2 * TOK), F32),
            pltpu.VMEM((LANES, 2, HD, 2 * TOK), F32),
            pltpu.VMEM((LANES, 2, HD, 2 * TOK), F32),
            stat, stat, stat,
            pltpu.VMEM((12, 2, TOK, HD), F32),
            pltpu.VMEM((8, 2, TOK, HD), BF16),
            pltpu.VMEM((4, 2, TOK, HD), BF16),
            pltpu.VMEM((4, 2, TOK, HD), BF16),
            pltpu.VMEM((4, 2, TOK, HD), BF16),
            pltpu.VMEM((LANES, TOK, WIDE), BF16),
            pltpu.VMEM((LANES, TOK, WIDE), BF16),
            dma((4,)), dma((3,)),
            dma((5, 3)), dma((5, 4)),
            dma((4,)), dma((4,)),
            dma((2,)), dma((2,)),
            dma((1,)), dma((1,)),
            dma((4,)), dma((4,)),
            dma((4,)), dma((4,)),
            dma((3, 3)), dma((3, 4)),
        ],
        compiler_params=pltpu.CompilerParams(
            collective_id=0, has_side_effects=True, vmem_limit_bytes=58 * 1024 * 1024),
    )(queries, keys, values, out_grad, docs.reshape(1, TOK))
    wide = pl.BlockSpec((1, TOK, WIDE), lambda i: (i, 0, 0))
    pair = pl.BlockSpec((1, 2, TOK, HD), lambda i: (i, 0, 0, 0))
    wide_out = pl.BlockSpec((TOK, WIDE), lambda i: (0, i))
    head_out = pl.BlockSpec((TOK, HD), lambda i: (0, i))
    return pl.pallas_call(
        finish,
        grid=(LANES,),
        out_shape=(
            jax.ShapeDtypeStruct((TOK, QH * HD), BF16),
            jax.ShapeDtypeStruct((TOK, QH * HD), F32),
            jax.ShapeDtypeStruct((TOK, KVH * HD), F32),
            jax.ShapeDtypeStruct((TOK, KVH * HD), F32),
        ),
        in_specs=[wide, wide, pair],
        out_specs=(wide_out, wide_out, head_out, head_out),
    )(*parts)


def solution(mesh):
    spec = P(("blk", "uly"), None)
    return jax.shard_map(
        on_device,
        mesh=mesh,
        in_specs=(spec, spec, spec, spec, P(("blk", "uly"))),
        out_specs=(spec, spec, spec, spec),
        check_vma=False,
    )
```

time: 148 us -> 53.5 us (0.36)
  the two profiles are of different devices: /device:TPU:384 before, /device:TPU:386 now
where the time goes in v2:
time: 53.5 us; the launch traced here: 53.3 us
  Pallas kernels  52.7 us (99%)
  between operations  0.64 us (1%)
    pallas_call x1, Pallas kernels, on_device(): pl.pallas_call(kernel, out_shape=(jax.ShapeDtypeStruct((LANES, TOK, WIDE)...  49 us
    pallas_call x1, Pallas kernels, on_device(): pl.pallas_call(finish, grid=(LANES,), out_shape=(jax.ShapeDtypeStruct((TO...  3.61 us

profile of v2, /device:TPU:386, one launch (start us, length us, event | category | flops | bytes accessed | tf_op | source)
XLA Modules:
  0.0 53.3 jit_solution(2388317425580451825)
XLA Ops:
  0.6 49.0 %shard_map.84 = (bf16[4,128,512]{2,1,0:T(8,128)(2,1)}, bf16[4,128,512]{2,1,0:T(8,128)(2,1)}, bf16[4,2,128,128]{3,2,1,0:T(8,128)(2,1)}) custom-call(bf16[128,2048]{1,0:T(8,128)(2,1)} %q_hbm.1, bf16[128,512]{1,0:T(8,128)(2,1)} %k_hbm.1, bf16[128,512]{1,0:T(8,128)(2,1)} %v_hbm.1, bf16[128,2048]{1,0:T(8,128)(2,1)} %g_hbm.1, s32[1,128]{1,0:T(1,128)} %bitcast.1), custom_call_target="tpu_custom_call" | custom-call | tf_op jit(solution)/shard_map/pallas_call | solution.py:372
  49.7 3.6 %shard_map.85 = (bf16[128,2048]{1,0:T(8,128)(2,1)}, f32[128,2048]{1,0:T(8,128)}, f32[128,512]{1,0:T(8,128)}, f32[128,512]{1,0:T(8,128)}) custom-call(bf16[4,128,512]{2,1,0:T(8,128)(2,1)} %get-tuple-element.7.o_ref, bf16[4,128,512]{2,1,0:T(8,128)(2,1)} %get-tuple-element.8.dq_ref, bf16[4,2,128,128]{3,2,1,0:T(8,128)(2,1)} %get-tuple-element.9.dkv_ref), custom_call_target="tpu_custom_call" | custom-call | tf_op jit(solution)/shard_map/pallas_call | solution.py:416

commit v3 on v2

--- a/solution.py
+++ b/solution.py
@@ -17,15 +17,16 @@
 C2 = HD ** -0.5 * math.log2(math.e)
 SCALE = HD ** -0.5
 LOW = -1e30
-NT = (((1,), (1,)), ((), ()))
 F32 = jnp.float32
 BF16 = jnp.bfloat16
 MESH = pl.DeviceIdType.MESH
 WIDE = GQ * HD
+FWD_STEP = 1
+BWD_STEP = 1
 
 
 def kernel(q_hbm, k_hbm, v_hbm, g_hbm, docs_ref, o_out, dq_out, dkv_out,
-           kv, kt, vt, dd, kd, qs, gs, s_ref, ot, dqt, m_ref, l_ref, dl_ref,
+           kv, kt, vt, dd, kd, qs, gs, qt, gt, s_ref, ds_ref, ot, m_ref, l_ref, dl_ref,
            da, ct, fin, rxs, rxy, o_buf, dq_buf,
            lsem, osem, asend, arecv, bsend, brecv, ssend, srecv, dsem, drecv,
            rssend, rsrecv, rysend, ryrecv, osend, orecv):
@@ -87,7 +88,7 @@
     dd[8 + x] = jnp.broadcast_to(docs_ref[...], (8, TOK))
     pl.semaphore_wait(barrier, 4 + jnp.where(blk < blks - 2, 1, 0) + jnp.where(blk >= 2, 1, 0))
 
-    for part in (0, 1, 2, 3):
+    for part in (0, 1, 2):
         for n in range(3):
             exchange(part, n).start()
 
@@ -114,11 +115,15 @@
     pl.when(blk < 2)(lambda: absent(0))
     pl.when(blk < 1)(lambda: absent(4))
 
+    for part in (0, 1):
+        for n in range(3):
+            exchange(part, n).wait_send()
+    for n in range(3):
+        exchange(3, n).start()
+
     m_ref[...] = jnp.full(m_ref.shape, LOW, F32)
     l_ref[...] = jnp.zeros(l_ref.shape, F32)
     ot[...] = jnp.zeros(ot.shape, F32)
-    dqt[...] = jnp.zeros(dqt.shape, F32)
-    da[...] = jnp.zeros(da.shape, F32)
 
     for n in (1, 2, 0):
         for part in (0, 1, 2):
@@ -131,9 +136,6 @@
         sibling_blocks(8).start()
         sibling_docs(8).start()
 
-    for n in range(3):
-        exchange(4, n).start()
-
     def prepare(row):
         for t in range(row, row + 4):
             kt[t] = kv[t, 0].T
@@ -141,6 +143,10 @@
             kd[t] = jnp.broadcast_to(dd[t][0:1], (TOK, TOK)).T
 
     prepare(8)
+    for n in range(3):
+        exchange(3, n).wait_send()
+    for n in range(3):
+        exchange(4, n).start()
     loads[2].wait()
     for n in range(3):
         exchanged(3, n)
@@ -174,30 +180,26 @@
     def tile(one_row, k, i):
         return jnp.where(one_row, 4 + k, jnp.where(i <= k, k, 9 + k))
 
-    def forward(index, carry):
-        @pl.when((index == 1) & (core == 0) | (index == 5) & (core == 1))
-        def _():
-            two_back()
-
-        @pl.when((index == 1) & (core == 1) | (index == 5) & (core == 0))
-        def _():
-            one_back()
-
-        phase = (index + 3) // 4
-        k = index - 1 - 4 * (phase - 1)
-        k = jnp.where(index == 0, -1, k)
-        one_row = (index > 0) & (lax.rem(phase + core, 2) == 0)
+    def stack(parts, axis=0):
+        return parts[0] if len(parts) == 1 else jnp.concatenate(parts, axis=axis)
+
+    def forward(one_row, ks):
         for i in range(LANES):
-            t = tile(one_row, k, i)
-            key_at = lax.broadcasted_iota(jnp.int32, (TOK, TOK), 0) + (t - 8 - i) * TOK
-            row_at = lax.broadcasted_iota(jnp.int32, (TOK, TOK), 1)
-            allowed = (kd[t] == dd[8 + i][0:1]) & (key_at <= row_at)
-            bias = jnp.where(allowed, 0.0, LOW).astype(F32)
-            bias = jnp.concatenate([bias, bias], axis=1)
+            tiles = [tile(one_row, k, i) for k in ks]
+            biases = []
+            for t in tiles:
+                key_at = lax.broadcasted_iota(jnp.int32, (TOK, TOK), 0) + (t - 8 - i) * TOK
+                row_at = lax.broadcasted_iota(jnp.int32, (TOK, TOK), 1)
+                allowed = (kd[t] == dd[8 + i][0:1]) & (key_at <= row_at)
+                bias = jnp.where(allowed, 0.0, LOW).astype(F32)
+                biases.append(jnp.concatenate([bias, bias], axis=1))
+            bias = stack(biases)
+            keys = stack([kv[t, 0] for t in tiles])
+            values_t = stack([vt[t] for t in tiles], 1)
             for p in range(2):
-                scores = lax.dot_general(
-                    kv[t, 0], heads(qs, i, p), NT, preferred_element_type=F32) * C2 + bias
-                s_ref[i, t - i, p] = scores
+                scores = jnp.dot(keys, qt[i, p], preferred_element_type=F32) * C2 + bias
+                for a, t in enumerate(tiles):
+                    s_ref[i, t - i, p] = scores[a * TOK:(a + 1) * TOK]
                 top = m_ref[i, p]
                 new_top = jnp.maximum(top, jnp.max(scores, axis=0, keepdims=True))
                 factor = jnp.exp2(top - new_top)
@@ -205,27 +207,50 @@
                 m_ref[i, p] = new_top
                 l_ref[i, p] = l_ref[i, p] * factor + jnp.sum(weights, axis=0, keepdims=True)
                 ot[i, p] = ot[i, p] * factor + jnp.dot(
-                    vt[t], weights.astype(BF16), preferred_element_type=F32)
+                    values_t, weights.astype(BF16), preferred_element_type=F32)
+
+    def forward_some(index, carry):
+        turns = 4 // FWD_STEP
+        at_start, at_middle = index == 0, index == turns
+
+        @pl.when(at_start & (core == 0) | at_middle & (core == 1))
+        def _():
+            two_back()
+
+        @pl.when(at_start & (core == 1) | at_middle & (core == 0))
+        def _():
+            one_back()
+
+        phase = index // turns
+        k = FWD_STEP * (index - turns * phase)
+        forward(lax.rem(phase + core, 2) == 1, tuple(k + a for a in range(FWD_STEP)))
         return carry
 
-    lax.fori_loop(0, TILES, forward, 0)
+    def turn(ref, out):
+        for i in range(LANES):
+            for p in range(2):
+                out[i, p] = heads(ref, i, p).T
+
+    turn(qs, qt)
+    forward(False, (-1,))
+    lax.fori_loop(0, 8 // FWD_STEP, forward_some, 0)
 
     loads[3].wait()
     for n in range(3):
         exchanged(4, n)
+
+    turn(gs, gt)
 
     for i in range(LANES):
         for p in range(2):
             total = l_ref[i, p]
             out = (ot[i, p] / total).astype(BF16)
             m_ref[i, p] = m_ref[i, p] + jnp.log2(total)
+            dl_ref[i, p] = jnp.sum(
+                gt[i, p].astype(F32) * out.astype(F32), axis=0, keepdims=True)
             for e in range(2):
                 lo = (2 * p + e) * HD
-                half = out[:, e * TOK:(e + 1) * TOK]
-                o_buf[i, :, lo:lo + HD] = half.T
-                grad_t = gs[i, :, lo:lo + HD].T.astype(F32)
-                dl_ref[i, p, :, e * TOK:(e + 1) * TOK] = jnp.sum(
-                    grad_t * half.astype(F32), axis=0, keepdims=True)
+                o_buf[i, :, lo:lo + HD] = out[:, e * TOK:(e + 1) * TOK].T
 
     def deliver(kind, n):
         peer = peers[n]
@@ -253,65 +278,89 @@
     def to_behind(k):
         return remote(ct.at[k], rxy.at[k], rysend.at[k], ryrecv.at[k], behind)
 
-    def step(n):
-        off = jnp.where(n == 0, 2, jnp.where(n == 1, 1, jnp.where(n == 2, 3, 0)))
-        return lax.rem(x + off, 4)
-
-    def backward(index, carry):
-        phase = index // 4
-        k = jnp.where(index == 8, -1, step(index - 4 * phase))
-        one_row = (index < 8) & (lax.rem(phase + core, 2) == 0)
+    def backward(one_row, ks):
+        zero = jnp.zeros((TOK, HD), F32)
+        early = [[zero, zero] for _ in ks]
+        total = [[zero, zero] for _ in ks]
         for i in range(LANES):
-            t = tile(one_row, k, i)
-            key_grad = jnp.zeros((TOK, HD), F32)
-            value_grad = jnp.zeros((TOK, HD), F32)
+            tiles = [tile(one_row, k, i) for k in ks]
+            values = stack([kv[t, 1] for t in tiles])
+            parts = [0, 0]
             for p in range(2):
                 query, grad = heads(qs, i, p), heads(gs, i, p)
-                probs = jnp.exp2(s_ref[i, t - i, p] - m_ref[i, p])
-                dprob = lax.dot_general(kv[t, 1], grad, NT, preferred_element_type=F32)
+                probs = jnp.exp2(stack([s_ref[i, t - i, p] for t in tiles]) - m_ref[i, p])
+                dprob = jnp.dot(values, gt[i, p], preferred_element_type=F32)
                 dscore = (probs * (dprob - dl_ref[i, p])).astype(BF16)
-                value_grad += jnp.dot(probs.astype(BF16), grad, preferred_element_type=F32)
-                key_grad += jnp.dot(dscore, query, preferred_element_type=F32)
-                dqt[i, p] += jnp.dot(kt[t], dscore, preferred_element_type=F32)
-            da[t, 0] += key_grad
-            da[t, 1] += value_grad
-
-        @pl.when(one_row)
-        def _():
-            ct[4 + k] = da[4 + k].astype(BF16)
-            when_before(lambda: to_sibling(k).start())
-
-        @pl.when((core == 0) & (phase == 1))
-        def _():
-            ct[k] = da[k].astype(BF16)
-            when_behind(lambda: to_behind(k).start())
-
-        @pl.when((core == 1) & (index >= 2) & (index < 6) & (blk >= 2))
-        def _():
-            j = step(index - 2)
-            to_sibling(j).wait_recv()
-            ct[j] = (da[j] + rxs[j].astype(F32)).astype(BF16)
-            to_behind(j).start()
+                parts[0] += jnp.dot(dscore, query, preferred_element_type=F32)
+                parts[1] += jnp.dot(probs.astype(BF16), grad, preferred_element_type=F32)
+                for a, t in enumerate(tiles):
+                    ds_ref[i, p, t - i] = dscore[a * TOK:(a + 1) * TOK]
+            for a, k in enumerate(ks):
+                for kind in range(2):
+                    total[a][kind] += parts[kind][a * TOK:(a + 1) * TOK]
+                    early[a][kind] = jnp.where(
+                        one_row | (i <= k), total[a][kind], early[a][kind])
+        for a, k in enumerate(ks):
+            there = jnp.where(one_row, 4 + k, jnp.where(k < 0, 8, k))
+            own = jnp.where(one_row, 4, k + 1)
+            for kind in range(2):
+                ct[there, kind] = early[a][kind].astype(BF16)
+                da[own, kind] = total[a][kind] - early[a][kind]
+
+    def backward_some(index, carry):
+        turns = 4 // BWD_STEP
+        phase = index // turns
+        k = BWD_STEP * (index - turns * phase)
+        ks = tuple(k + a for a in range(BWD_STEP))
+        one_row = lax.rem(phase + core, 2) == 0
+        backward(one_row, ks)
+
+        @pl.when(one_row & (blk >= 1))
+        def _():
+            for j in ks:
+                to_sibling(j).start()
+
+        @pl.when((core == 0) & (phase == 1) & (blk >= 2))
+        def _():
+            for j in ks:
+                to_behind(j).start()
+
+        lag = 2 // BWD_STEP
+
+        @pl.when((core == 1) & (index >= lag) & (index < lag + turns) & (blk >= 2))
+        def _():
+            for a in range(BWD_STEP):
+                j = BWD_STEP * (index - lag) + a
+                to_sibling(j).wait_recv()
+                ct[j] = (ct[j].astype(F32) + rxs[j].astype(F32)).astype(BF16)
+                to_behind(j).start()
 
         return carry
 
-    lax.fori_loop(0, TILES, backward, 0)
-
-    for i in range(LANES):
+    lax.fori_loop(0, 8 // BWD_STEP, backward_some, 0)
+    backward(False, (-1,))
+
+    def query_grads(i):
+        keys_t = jnp.concatenate([kt[i + w] for w in range(TILES)], axis=1)
         for p in range(2):
+            grad_t = jnp.dot(
+                keys_t, ds_ref[i, p].reshape(TILES * TOK, 2 * TOK), preferred_element_type=F32)
             for e in range(2):
                 lo = (2 * p + e) * HD
                 dq_buf[i, :, lo:lo + HD] = (
-                    dqt[i, p, :, e * TOK:(e + 1) * TOK].T * SCALE).astype(BF16)
+                    grad_t[:, e * TOK:(e + 1) * TOK].T * SCALE).astype(BF16)
+
+    for n in range(3):
+        query_grads(peers[n])
+        deliver(1, n).start()
+    query_grads(x)
     keep[1].start()
-    for n in range(3):
-        deliver(1, n).start()
 
     @when_core0
     def _():
         for k in range(4):
             to_sibling(k).wait_recv()
-            da[8 + k] += rxs[k].astype(F32)
+            da[k] += rxs[k].astype(F32)
 
     for n in range(4):
         k = (peers + (x,))[n]
@@ -319,14 +368,14 @@
         @when_ahead
         def _():
             to_behind(k).wait_recv()
-            da[8 + k] += rxy[k].astype(F32)
-
-        fin[k] = da[8 + k].astype(BF16)
+            da[k] += rxy[k].astype(F32)
+
+        fin[k] = da[k].astype(BF16)
         if n < 3:
             deliver(2, n).start()
     keep[2].start()
 
-    for part in range(5):
+    for part in (2, 4):
         for n in range(3):
             exchange(part, n).wait_send()
     for kind in range(3):
@@ -357,11 +406,35 @@
             to_behind(k).wait_send()
 
 
-def finish(o_ref, dq_ref, dkv_ref, o_out, dq_out, dk_out, dv_out):
-    o_out[...] = o_ref[0]
-    dq_out[...] = dq_ref[0].astype(F32)
-    dk_out[...] = dkv_ref[0, 0].astype(F32) * SCALE
-    dv_out[...] = dkv_ref[0, 1].astype(F32)
+def finish(o_ref, dq_ref, dkv_ref, o_out, dq_out, dk_out, dv_out,
+           o_in, dq_in, dkv_in, dq_f32, dkv_f32, in_sem, out_sem):
+    wide = [slice(g * WIDE, (g + 1) * WIDE) for g in range(LANES)]
+    dq_loads = [pltpu.make_async_copy(dq_ref.at[g], dq_in.at[g], in_sem.at[g]) for g in range(4)]
+    dkv_load = pltpu.make_async_copy(dkv_ref, dkv_in, in_sem.at[4])
+    o_loads = [pltpu.make_async_copy(o_ref.at[g], o_in.at[g], in_sem.at[5 + g]) for g in range(4)]
+    stores = [pltpu.make_async_copy(dq_f32.at[g], dq_out.at[:, wide[g]], out_sem.at[g])
+              for g in range(LANES)]
+    stores.append(pltpu.make_async_copy(dkv_f32.at[0], dk_out, out_sem.at[4]))
+    stores.append(pltpu.make_async_copy(dkv_f32.at[1], dv_out, out_sem.at[5]))
+    stores += [pltpu.make_async_copy(o_in.at[g], o_out.at[:, wide[g]], out_sem.at[6 + g])
+               for g in range(LANES)]
+    for copy in dq_loads + [dkv_load] + o_loads:
+        copy.start()
+    for g in range(LANES):
+        dq_loads[g].wait()
+        dq_f32[g] = dq_in[g].astype(F32)
+        stores[g].start()
+    dkv_load.wait()
+    for g in range(KVH):
+        dkv_f32[0, :, g * HD:(g + 1) * HD] = dkv_in[g, 0].astype(F32) * SCALE
+        dkv_f32[1, :, g * HD:(g + 1) * HD] = dkv_in[g, 1].astype(F32)
+    for copy in stores[4:6]:
+        copy.start()
+    for g in range(LANES):
+        o_loads[g].wait()
+        stores[6 + g].start()
+    for copy in stores:
+        copy.wait()
 
 
 def on_device(queries, keys, values, out_grad, docs):
@@ -386,12 +459,14 @@
             pltpu.VMEM((12, TOK, TOK), jnp.int32),
             pltpu.VMEM((LANES, TOK, WIDE), BF16),
             pltpu.VMEM((LANES, TOK, WIDE), BF16),
+            pltpu.VMEM((LANES, 2, HD, 2 * TOK), BF16),
+            pltpu.VMEM((LANES, 2, HD, 2 * TOK), BF16),
             pltpu.VMEM((LANES, TILES, 2, TOK, 2 * TOK), F32),
-            pltpu.VMEM((LANES, 2, HD, 2 * TOK), F32),
+            pltpu.VMEM((LANES, 2, TILES, TOK, 2 * TOK), BF16),
             pltpu.VMEM((LANES, 2, HD, 2 * TOK), F32),
             stat, stat, stat,
-            pltpu.VMEM((12, 2, TOK, HD), F32),
-            pltpu.VMEM((8, 2, TOK, HD), BF16),
+            pltpu.VMEM((5, 2, TOK, HD), F32),
+            pltpu.VMEM((9, 2, TOK, HD), BF16),
             pltpu.VMEM((4, 2, TOK, HD), BF16),
             pltpu.VMEM((4, 2, TOK, HD), BF16),
             pltpu.VMEM((4, 2, TOK, HD), BF16),
@@ -409,21 +484,24 @@
         compiler_params=pltpu.CompilerParams(
             collective_id=0, has_side_effects=True, vmem_limit_bytes=58 * 1024 * 1024),
     )(queries, keys, values, out_grad, docs.reshape(1, TOK))
-    wide = pl.BlockSpec((1, TOK, WIDE), lambda i: (i, 0, 0))
-    pair = pl.BlockSpec((1, 2, TOK, HD), lambda i: (i, 0, 0, 0))
-    wide_out = pl.BlockSpec((TOK, WIDE), lambda i: (0, i))
-    head_out = pl.BlockSpec((TOK, HD), lambda i: (0, i))
     return pl.pallas_call(
         finish,
-        grid=(LANES,),
         out_shape=(
             jax.ShapeDtypeStruct((TOK, QH * HD), BF16),
             jax.ShapeDtypeStruct((TOK, QH * HD), F32),
             jax.ShapeDtypeStruct((TOK, KVH * HD), F32),
             jax.ShapeDtypeStruct((TOK, KVH * HD), F32),
         ),
-        in_specs=[wide, wide, pair],
-        out_specs=(wide_out, wide_out, head_out, head_out),
+        in_specs=[any_spec] * 3,
+        out_specs=(any_spec,) * 4,
+        scratch_shapes=[
+            pltpu.VMEM((LANES, TOK, WIDE), BF16),
+            pltpu.VMEM((LANES, TOK, WIDE), BF16),
+            pltpu.VMEM((KVH, 2, TOK, HD), BF16),
+            pltpu.VMEM((LANES, TOK, WIDE), F32),
+            pltpu.VMEM((2, TOK, KVH * HD), F32),
+            dma((9,)), dma((10,)),
+        ],
     )(*parts)
 
 

time: 53.5 us -> 49.2 us (0.920)
  the two profiles are of different devices: /device:TPU:386 before, /device:TPU:384 now
where the time goes in v3:
time: 49.2 us; the launch traced here: 48.9 us
  Pallas kernels  48.3 us (98%)
  between operations  0.64 us (1%)
    pallas_call x1, Pallas kernels, on_device(): pl.pallas_call(kernel, out_shape=(jax.ShapeDtypeStruct((LANES, TOK, WIDE)...  45.9 us
    pallas_call x1, Pallas kernels, on_device(): pl.pallas_call(finish, out_shape=(jax.ShapeDtypeStruct((TOK, QH * HD), BF...  2.4 us

profile of v3, /device:TPU:384, one launch (start us, length us, event | category | flops | bytes accessed | tf_op | source)
XLA Modules:
  0.0 48.9 jit_solution(7848733717627739600)
XLA Ops:
  0.6 45.9 %shard_map.84 = (bf16[4,128,512]{2,1,0:T(8,128)(2,1)}, bf16[4,128,512]{2,1,0:T(8,128)(2,1)}, bf16[4,2,128,128]{3,2,1,0:T(8,128)(2,1)}) custom-call(bf16[128,2048]{1,0:T(8,128)(2,1)} %q_hbm.1, bf16[128,512]{1,0:T(8,128)(2,1)} %k_hbm.1, bf16[128,512]{1,0:T(8,128)(2,1)} %v_hbm.1, bf16[128,2048]{1,0:T(8,128)(2,1)} %g_hbm.1, s32[1,128]{1,0:T(1,128)} %bitcast.1), custom_call_target="tpu_custom_call" | custom-call | tf_op jit(solution)/shard_map/pallas_call | solution.py:445
  46.5 2.4 %shard_map.85 = (bf16[128,2048]{1,0:T(8,128)(2,1)}, f32[128,2048]{1,0:T(8,128)}, f32[128,512]{1,0:T(8,128)}, f32[128,512]{1,0:T(8,128)}) custom-call(bf16[4,128,512]{2,1,0:T(8,128)(2,1)} %get-tuple-element.7.o_ref, bf16[4,128,512]{2,1,0:T(8,128)(2,1)} %get-tuple-element.8.dq_ref, bf16[4,2,128,128]{3,2,1,0:T(8,128)(2,1)} %get-tuple-element.9.dkv_ref), custom_call_target="tpu_custom_call" | custom-call | tf_op jit(solution)/shard_map/pallas_call | solution.py:487

commit v4 on v3

v4 whole, which is shorter than its diff:
```python
import math

import jax
import jax.numpy as jnp
from jax import lax
from jax.experimental import pallas as pl
from jax.experimental.pallas import tpu as pltpu
from jax.sharding import PartitionSpec as P

HD = 128
KVH = 4
QH = 16
GQ = 4
TOK = 128
LANES = 4
TILES = 9
C2 = HD ** -0.5 * math.log2(math.e)
SCALE = HD ** -0.5
LOW = -1e30
F32 = jnp.float32
BF16 = jnp.bfloat16
MESH = pl.DeviceIdType.MESH
WIDE = GQ * HD


def kernel(q_hbm, k_hbm, v_hbm, g_hbm, docs_ref, o_out, dq_out, dkv_out,
           kv, kt, vt, dd, kd, qs, gs, qt, gt, s_ref, dp_ref, wb, pb, dsb, ot, m_ref,
           acc, ct, fin, rxs, rxy, o_buf, dq_buf,
           lsem, osem, asend, arecv, bsend, brecv, ssend, srecv, dsem, drecv,
           rssend, rsrecv, rysend, ryrecv, osend, orecv):
    x = lax.axis_index("uly")
    blk = lax.axis_index("blk")
    blks = lax.axis_size("blk")
    core = lax.rem(blk, 2)
    peers = tuple(lax.rem(x + k, 4) for k in (2, 1, 3))
    ahead, behind = {"blk": blk + 2}, {"blk": blk - 2}
    sibling = {"blk": blk + 1 - 2 * core}
    when_ahead, when_behind = pl.when(blk < blks - 2), pl.when(blk >= 2)
    when_before = pl.when(blk >= 1)
    when_core0, when_core1 = pl.when(core == 0), pl.when(core == 1)

    def cols(index, width):
        return pl.ds(pl.multiple_of(index * width, width), width)

    def remote(src, dst, send_sem, recv_sem, dev):
        return pltpu.make_async_remote_copy(
            src_ref=src, dst_ref=dst, send_sem=send_sem, recv_sem=recv_sem,
            device_id=dev, device_id_type=MESH)

    def exchange(part, n):
        peer = peers[n]
        src, dst = (
            (k_hbm.at[:, cols(peer, HD)], kv.at[8 + x, 0]),
            (v_hbm.at[:, cols(peer, HD)], kv.at[8 + x, 1]),
            (dd.at[8 + x], dd.at[8 + x]),
            (q_hbm.at[:, cols(peer, WIDE)], qs.at[x]),
            (g_hbm.at[:, cols(peer, WIDE)], gs.at[x]),
        )[part]
        return remote(src, dst, asend.at[part, n], arecv.at[part, x], {"uly": peer})

    def exchanged(part, n):
        origin = peers[n]
        dst = (kv.at[8 + origin, 0], kv.at[8 + origin, 1], dd.at[8 + origin],
               qs.at[origin], gs.at[origin])[part]
        remote(dst, dst, asend.at[part, n], arecv.at[part, origin], {"uly": origin}).wait_recv()

    loads = [
        pltpu.make_async_copy(k_hbm.at[:, cols(x, HD)], kv.at[8 + x, 0], lsem.at[0]),
        pltpu.make_async_copy(v_hbm.at[:, cols(x, HD)], kv.at[8 + x, 1], lsem.at[1]),
        pltpu.make_async_copy(q_hbm.at[:, cols(x, WIDE)], qs.at[x], lsem.at[2]),
        pltpu.make_async_copy(g_hbm.at[:, cols(x, WIDE)], gs.at[x], lsem.at[3]),
    ]
    for load in loads:
        load.start()

    barrier = pltpu.get_barrier_semaphore()

    def greet(dev):
        pl.semaphore_signal(barrier, inc=1, device_id=dev, device_id_type=MESH)

    for peer in peers:
        greet({"uly": peer})
    greet(sibling)
    for k in range(LANES):
        when_ahead(lambda: greet({"blk": blk + 2, "uly": k}))
        when_behind(lambda: greet({"blk": blk - 2, "uly": k}))
    dd[8 + x] = jnp.broadcast_to(docs_ref[...], (8, TOK))
    pl.semaphore_wait(barrier, 4 + jnp.where(blk < blks - 2, 4, 0) + jnp.where(blk >= 2, 4, 0))

    for part in (0, 1, 2):
        for n in range(3):
            exchange(part, n).start()

    def forward_block(k):
        return remote(kv.at[8 + k], kv.at[k], bsend.at[k], brecv.at[k], ahead)

    def forward_docs():
        return remote(dd.at[8:12], dd.at[0:4], dsem.at[0], drecv.at[0], ahead)

    def sibling_blocks(row):
        return remote(kv.at[pl.ds(row, 4)], kv.at[4:8], ssend.at[0], srecv.at[0], sibling)

    def sibling_docs(row):
        return remote(dd.at[pl.ds(row, 4)], dd.at[4:8], ssend.at[1], srecv.at[1], sibling)

    loads[0].wait()
    loads[1].wait()
    when_ahead(lambda: forward_block(x).start())

    def absent(row):
        kv[row:row + 4] = jnp.zeros((4, 2, TOK, HD), BF16)
        dd[row:row + 4] = jnp.full((4, 8, TOK), -1, jnp.int32)

    pl.when(blk < 2)(lambda: absent(0))
    pl.when(blk < 1)(lambda: absent(4))

    for part in (0, 1):
        for n in range(3):
            exchange(part, n).wait_send()
    for n in range(3):
        exchange(3, n).start()

    acc[...] = jnp.zeros(acc.shape, F32)

    for n in (1, 2, 0):
        for part in (0, 1, 2):
            exchanged(part, n)
        when_ahead(lambda: forward_block(peers[n]).start())
    when_ahead(lambda: forward_docs().start())

    @when_core0
    def _():
        sibling_blocks(8).start()
        sibling_docs(8).start()

    def prepare(row):
        for t in range(row, row + 4):
            vt[t] = kv[t, 1].T
            kd[t] = jnp.broadcast_to(dd[t][0:1], (TOK, TOK)).T

    prepare(8)
    for n in range(3):
        exchange(3, n).wait_send()
    for n in range(3):
        exchange(4, n).start()
    loads[2].wait()
    for n in range(3):
        exchanged(3, n)

    def two_back():
        @when_behind
        def _():
            for k in range(4):
                remote(kv.at[k], kv.at[k], bsend.at[k], brecv.at[k], behind).wait_recv()
            forward_docs().wait_recv()

            @when_core1
            def _():
                sibling_blocks(0).start()
                sibling_docs(0).start()

        prepare(0)

    def one_back():
        @when_before
        def _():
            sibling_blocks(0).wait_recv()
            sibling_docs(0).wait_recv()

        prepare(4)

    def heads(ref, i, p):
        lo = 2 * p * HD
        return jnp.concatenate([ref[i, :, lo:lo + HD], ref[i, :, lo + HD:lo + 2 * HD]], axis=0)

    def turn(ref, out):
        for i in range(LANES):
            for p in range(2):
                out[i, p] = heads(ref, i, p).T

    def step(n):
        off = jnp.where(n == 0, 2, jnp.where(n == 1, 1, jnp.where(n == 2, 3, 0)))
        return lax.rem(x + off, 4)

    def deliver(kind, n, peer):
        src, dst = ((o_buf.at[peer], o_out.at[x]), (dq_buf.at[peer], dq_out.at[x]),
                    (fin.at[peer], dkv_out.at[x]))[kind]
        return remote(src, dst, osend.at[kind, n], orecv.at[kind, x], {"uly": peer})

    def delivered(kind, n):
        origin = peers[n]
        dst = (o_out, dq_out, dkv_out)[kind].at[origin]
        remote(dst, dst, osend.at[kind, n], orecv.at[kind, origin], {"uly": origin}).wait_recv()

    keep = [
        pltpu.make_async_copy(o_buf.at[x], o_out.at[x], osem.at[0]),
        pltpu.make_async_copy(dq_buf.at[x], dq_out.at[x], osem.at[1]),
        pltpu.make_async_copy(fin.at[x], dkv_out.at[x], osem.at[2]),
    ]

    def window(ref, i):
        return jnp.concatenate([ref[i + w] for w in range(TILES)], axis=1)

    def over_rows(part, op):
        return op(part.reshape(TOK // 8, 8, 2 * TOK), axis=0)

    def forward(n, carry):
        i = step(n)
        keys = kv[pl.ds(i, TILES), 0].reshape(TILES * TOK, HD)
        values_t = window(vt, i)
        for p in range(2):
            s_ref[i, p] = jnp.dot(
                keys, qt[i, p], preferred_element_type=F32).reshape(TILES, TOK, 2 * TOK)
        docs_row = dd[8 + i][0:1]
        key_at = lax.broadcasted_iota(jnp.int32, (TOK, TOK), 0)
        row_at = lax.broadcasted_iota(jnp.int32, (TOK, TOK), 1)
        tops, sums = [None, None], [None, None]
        for w in range(TILES):
            allowed = kd[i + w] == docs_row
            if w == TILES - 1:
                allowed = allowed & (key_at <= row_at)
            bias = jnp.where(allowed, 0.0, LOW).astype(F32)
            bias = jnp.concatenate([bias, bias], axis=1)
            for p in range(2):
                scores = s_ref[i, p, w] * C2 + bias
                s_ref[i, p, w] = scores
                part = over_rows(scores, jnp.max)
                tops[p] = part if w == 0 else jnp.maximum(tops[p], part)
        for p in range(2):
            tops[p] = jnp.max(tops[p], axis=0, keepdims=True)
        for w in range(TILES):
            for p in range(2):
                weights = jnp.exp2(s_ref[i, p, w] - tops[p])
                part = over_rows(weights, jnp.sum)
                sums[p] = part if w == 0 else sums[p] + part
                wb[p, w] = weights.astype(BF16)
        for p in range(2):
            total = jnp.sum(sums[p], axis=0, keepdims=True)
            out = jnp.dot(values_t, wb[p].reshape(TILES * TOK, 2 * TOK),
                          preferred_element_type=F32)
            out = (out / total).astype(BF16)
            ot[i, p] = out
            m_ref[i, p] = tops[p] + jnp.log2(total)
            for e in range(2):
                lo = (2 * p + e) * HD
                o_buf[i, :, lo:lo + HD] = out[:, e * TOK:(e + 1) * TOK].T
        pl.when(n < 3)(lambda: deliver(0, n, i).start())
        return carry

    turn(qs, qt)
    two_back()
    one_back()
    lax.fori_loop(0, LANES, forward, 0)
    keep[0].start()
    for t in range(12):
        kt[t] = kv[t, 0].T
    loads[3].wait()

    def backward(n, carry):
        i = lax.rem(x + jnp.where(n == 0, 0, jnp.where(n == 1, 2, jnp.where(n == 2, 1, 3))), 4)
        for m in range(3):
            pl.when(n == m + 1)(lambda: exchanged(4, m))
        for p in range(2):
            gt[i, p] = heads(gs, i, p).T
        values = kv[pl.ds(i, TILES), 1].reshape(TILES * TOK, HD)
        keys_t = window(kt, i)
        deltas = []
        for p in range(2):
            dp_ref[p] = jnp.dot(
                values, gt[i, p], preferred_element_type=F32).reshape(TILES, TOK, 2 * TOK)
            deltas.append(jnp.sum(
                gt[i, p].astype(F32) * ot[i, p].astype(F32), axis=0, keepdims=True))
        for w in range(TILES):
            for p in range(2):
                rows = slice(p * 2 * TOK, (p + 1) * 2 * TOK)
                probs = jnp.exp2(s_ref[i, p, w] - m_ref[i, p])
                pb[w, :, rows] = probs.astype(BF16)
                dsb[w, :, rows] = (probs * (dp_ref[p, w] - deltas[p])).astype(BF16)
        for kind, (left_ref, right_ref) in enumerate(((dsb, qs), (pb, gs))):
            rows = jnp.concatenate([heads(right_ref, i, 0), heads(right_ref, i, 1)], axis=0)
            acc[pl.ds(i, TILES), kind] += jnp.dot(
                left_ref[...].reshape(TILES * TOK, WIDE), rows,
                preferred_element_type=F32).reshape(TILES, TOK, HD)
        for p in range(2):
            grad_t = jnp.dot(
                keys_t, dsb[:, :, p * 2 * TOK:(p + 1) * 2 * TOK].reshape(TILES * TOK, 2 * TOK),
                preferred_element_type=F32)
            for e in range(2):
                lo = (2 * p + e) * HD
                dq_buf[i, :, lo:lo + HD] = (
                    grad_t[:, e * TOK:(e + 1) * TOK].T * SCALE).astype(BF16)
        pl.when(n > 0)(lambda: deliver(1, n - 1, i).start())
        return carry

    def to_sibling(k):
        return remote(ct.at[4 + k], rxs.at[k], rssend.at[k], rsrecv.at[k], sibling)

    def to_behind(k):
        return remote(ct.at[k], dkv_out.at[4 + x], rysend.at[k], ryrecv.at[x],
                      {"blk": blk - 2, "uly": k})

    def from_ahead(k):
        dst = dkv_out.at[4 + k]
        remote(dst, dst, rysend.at[k], ryrecv.at[k], {"blk": blk + 2, "uly": k}).wait_recv()

    lax.fori_loop(0, LANES, backward, 0)
    keep[1].start()

    home = peers + (x,)

    @when_before
    def _():
        for k in home:
            ct[4 + k] = acc[4 + k].astype(BF16)
            to_sibling(k).start()

    @pl.when((core == 0) & (blk >= 2))
    def _():
        for k in home:
            ct[k] = acc[k].astype(BF16)
            to_behind(k).start()

    @pl.when((core == 1) & (blk >= 2))
    def _():
        for k in home:
            to_sibling(k).wait_recv()
            ct[k] = (acc[k] + rxs[k].astype(F32)).astype(BF16)
            to_behind(k).start()

    @when_core0
    def _():
        for k in range(4):
            to_sibling(k).wait_recv()
            acc[8 + k] += rxs[k].astype(F32)

    for n in range(4):
        k = home[n]
        fin[k] = acc[8 + k].astype(BF16)
        if n < 3:
            deliver(2, n, k).start()
    keep[2].start()

    @when_ahead
    def _():
        for k in range(4):
            from_ahead(k)

    @pl.when(blk >= blks - 2)
    def _():
        none_ahead = pltpu.make_async_copy(rxy, dkv_out.at[4:8], osem.at[3])
        rxy[...] = jnp.zeros(rxy.shape, BF16)
        none_ahead.start()
        none_ahead.wait()

    for part in (2, 4):
        for n in range(3):
            exchange(part, n).wait_send()
    for kind in range(3):
        for n in range(3):
            delivered(kind, n)
            deliver(kind, n, peers[n]).wait_send()
        keep[kind].wait()

    @when_ahead
    def _():
        for k in range(4):
            forward_block(k).wait_send()
        forward_docs().wait_send()

    @pl.when(blk != 1)
    def _():
        sibling_blocks(0).wait_send()
        sibling_docs(0).wait_send()

    @when_before
    def _():
        for k in range(4):
            to_sibling(k).wait_send()

    @when_behind
    def _():
        for k in range(4):
            to_behind(k).wait_send()


def finish(o_ref, dq_ref, dkv_ref, o_out, dq_out, dk_out, dv_out,
           o_in, dq_in, dkv_in, dq_f32, dkv_f32, in_sem, out_sem):
    wide = [slice(g * WIDE, (g + 1) * WIDE) for g in range(LANES)]
    dq_loads = [pltpu.make_async_copy(dq_ref.at[g], dq_in.at[g], in_sem.at[g]) for g in range(4)]
    dkv_load = pltpu.make_async_copy(dkv_ref, dkv_in, in_sem.at[4])
    o_loads = [pltpu.make_async_copy(o_ref.at[g], o_in.at[g], in_sem.at[5 + g]) for g in range(4)]
    stores = [pltpu.make_async_copy(dq_f32.at[g], dq_out.at[:, wide[g]], out_sem.at[g])
              for g in range(LANES)]
    stores.append(pltpu.make_async_copy(dkv_f32.at[0], dk_out, out_sem.at[4]))
    stores.append(pltpu.make_async_copy(dkv_f32.at[1], dv_out, out_sem.at[5]))
    stores += [pltpu.make_async_copy(o_in.at[g], o_out.at[:, wide[g]], out_sem.at[6 + g])
               for g in range(LANES)]
    for copy in dq_loads + [dkv_load] + o_loads:
        copy.start()
    for g in range(LANES):
        dq_loads[g].wait()
        dq_f32[g] = dq_in[g].astype(F32)
        stores[g].start()
    dkv_load.wait()
    for g in range(KVH):
        cols = slice(g * HD, (g + 1) * HD)
        key_grad, value_grad = (
            dkv_in[g, kind].astype(F32) + dkv_in[4 + g, kind].astype(F32) for kind in range(2))
        dkv_f32[0, :, cols] = key_grad * SCALE
        dkv_f32[1, :, cols] = value_grad
    for copy in stores[4:6]:
        copy.start()
    for g in range(LANES):
        o_loads[g].wait()
        stores[6 + g].start()
    for copy in stores:
        copy.wait()


def on_device(queries, keys, values, out_grad, docs):
    any_spec = pl.BlockSpec(memory_space=pl.ANY)
    vmem_spec = pl.BlockSpec(memory_space=pltpu.VMEM)
    dma = pltpu.SemaphoreType.DMA
    parts = pl.pallas_call(
        kernel,
        out_shape=(
            jax.ShapeDtypeStruct((LANES, TOK, WIDE), BF16),
            jax.ShapeDtypeStruct((LANES, TOK, WIDE), BF16),
            jax.ShapeDtypeStruct((2 * LANES, 2, TOK, HD), BF16),
        ),
        in_specs=[any_spec] * 4 + [vmem_spec],
        out_specs=(any_spec,) * 3,
        scratch_shapes=[
            pltpu.VMEM((12, 2, TOK, HD), BF16),
            pltpu.VMEM((12, HD, TOK), BF16),
            pltpu.VMEM((12, HD, TOK), BF16),
            pltpu.VMEM((12, 8, TOK), jnp.int32),
            pltpu.VMEM((12, TOK, TOK), jnp.int32),
            pltpu.VMEM((LANES, TOK, WIDE), BF16),
            pltpu.VMEM((LANES, TOK, WIDE), BF16),
            pltpu.VMEM((LANES, 2, HD, 2 * TOK), BF16),
            pltpu.VMEM((LANES, 2, HD, 2 * TOK), BF16),
            pltpu.VMEM((LANES, 2, TILES, TOK, 2 * TOK), F32),
            pltpu.VMEM((2, TILES, TOK, 2 * TOK), F32),
            pltpu.VMEM((2, TILES, TOK, 2 * TOK), BF16),
            pltpu.VMEM((TILES, TOK, WIDE), BF16),
            pltpu.VMEM((TILES, TOK, WIDE), BF16),
            pltpu.VMEM((LANES, 2, HD, 2 * TOK), BF16),
            pltpu.VMEM((LANES, 2, 1, 2 * TOK), F32),
            pltpu.VMEM((12, 2, TOK, HD), F32),
            pltpu.VMEM((8, 2, TOK, HD), BF16),
            pltpu.VMEM((4, 2, TOK, HD), BF16),
            pltpu.VMEM((4, 2, TOK, HD), BF16),
            pltpu.VMEM((4, 2, TOK, HD), BF16),
            pltpu.VMEM((LANES, TOK, WIDE), BF16),
            pltpu.VMEM((LANES, TOK, WIDE), BF16),
            dma((4,)), dma((4,)),
            dma((5, 3)), dma((5, 4)),
            dma((4,)), dma((4,)),
            dma((2,)), dma((2,)),
            dma((1,)), dma((1,)),
            dma((4,)), dma((4,)),
            dma((4,)), dma((4,)),
            dma((3, 3)), dma((3, 4)),
        ],
        compiler_params=pltpu.CompilerParams(
            collective_id=0, has_side_effects=True, vmem_limit_bytes=58 * 1024 * 1024),
    )(queries, keys, values, out_grad, docs.reshape(1, TOK))
    return pl.pallas_call(
        finish,
        out_shape=(
            jax.ShapeDtypeStruct((TOK, QH * HD), BF16),
            jax.ShapeDtypeStruct((TOK, QH * HD), F32),
            jax.ShapeDtypeStruct((TOK, KVH * HD), F32),
            jax.ShapeDtypeStruct((TOK, KVH * HD), F32),
        ),
        in_specs=[any_spec] * 3,
        out_specs=(any_spec,) * 4,
        scratch_shapes=[
            pltpu.VMEM((LANES, TOK, WIDE), BF16),
            pltpu.VMEM((LANES, TOK, WIDE), BF16),
            pltpu.VMEM((2 * KVH, 2, TOK, HD), BF16),
            pltpu.VMEM((LANES, TOK, WIDE), F32),
            pltpu.VMEM((2, TOK, KVH * HD), F32),
            dma((9,)), dma((10,)),
        ],
    )(*parts)


def solution(mesh):
    spec = P(("blk", "uly"), None)
    return jax.shard_map(
        on_device,
        mesh=mesh,
        in_specs=(spec, spec, spec, spec, P(("blk", "uly"))),
        out_specs=(spec, spec, spec, spec),
        check_vma=False,
    )
```

time: 49.2 us -> 45.6 us (0.927)
  Pallas kernels: 48.3 us -> 44.8 us
    pallas_call x1, Pallas kernels: 45.9 us -> 42.3 us  [on_device(): pl.pallas_call(kernel, out_shape=(jax.ShapeDtypeStruct((LANES, TOK, WIDE)...]
where the time goes in v4:
time: 45.6 us; the launch traced here: 45.4 us
  Pallas kernels  44.8 us (98%)
  between operations  0.64 us (1%)
    pallas_call x1, Pallas kernels, on_device(): pl.pallas_call(kernel, out_shape=(jax.ShapeDtypeStruct((LANES, TOK, WIDE)...  42.3 us
    pallas_call x1, Pallas kernels, on_device(): pl.pallas_call(finish, out_shape=(jax.ShapeDtypeStruct((TOK, QH * HD), BF...  2.51 us

profile of v4, /device:TPU:384, one launch (start us, length us, event | category | flops | bytes accessed | tf_op | source)
XLA Modules:
  0.0 45.4 jit_solution(12450781933991467738)
XLA Ops:
  0.6 42.3 %shard_map.84 = (bf16[4,128,512]{2,1,0:T(8,128)(2,1)}, bf16[4,128,512]{2,1,0:T(8,128)(2,1)}, bf16[8,2,128,128]{3,2,1,0:T(8,128)(2,1)}) custom-call(bf16[128,2048]{1,0:T(8,128)(2,1)} %q_hbm.1, bf16[128,512]{1,0:T(8,128)(2,1)} %k_hbm.1, bf16[128,512]{1,0:T(8,128)(2,1)} %v_hbm.1, bf16[128,2048]{1,0:T(8,128)(2,1)} %g_hbm.1, s32[1,128]{1,0:T(1,128)} %bitcast.1), custom_call_target="tpu_custom_call" | custom-call | tf_op jit(solution)/shard_map/pallas_call | solution.py:424
  42.9 2.5 %shard_map.85 = (bf16[128,2048]{1,0:T(8,128)(2,1)}, f32[128,2048]{1,0:T(8,128)}, f32[128,512]{1,0:T(8,128)}, f32[128,512]{1,0:T(8,128)}) custom-call(bf16[4,128,512]{2,1,0:T(8,128)(2,1)} %get-tuple-element.7.o_ref, bf16[4,128,512]{2,1,0:T(8,128)(2,1)} %get-tuple-element.8.dq_ref, bf16[8,2,128,128]{3,2,1,0:T(8,128)(2,1)} %get-tuple-element.9.dkv_ref), custom_call_target="tpu_custom_call" | custom-call | tf_op jit(solution)/shard_map/pallas_call | solution.py:469

commit v5 on v4

--- a/solution.py
+++ b/solution.py
@@ -320,6 +320,15 @@
             ct[k] = acc[k].astype(BF16)
             to_behind(k).start()
 
+    def own_grads():
+        for n in range(4):
+            k = home[n]
+            fin[k] = acc[8 + k].astype(BF16)
+            if n < 3:
+                deliver(2, n, k).start()
+
+    when_core1(own_grads)
+
     @pl.when((core == 1) & (blk >= 2))
     def _():
         for k in home:
@@ -332,12 +341,8 @@
         for k in range(4):
             to_sibling(k).wait_recv()
             acc[8 + k] += rxs[k].astype(F32)
-
-    for n in range(4):
-        k = home[n]
-        fin[k] = acc[8 + k].astype(BF16)
-        if n < 3:
-            deliver(2, n, k).start()
+        own_grads()
+
     keep[2].start()
 
     @when_ahead

time: 45.6 us -> 45.6 us (level)
  no operation moved by 1% of the time
where the time goes in v5:
time: 45.6 us; the launch traced here: 45.4 us
  Pallas kernels  44.8 us (98%)
  between operations  0.64 us (1%)
    pallas_call x1, Pallas kernels, on_device(): pl.pallas_call(kernel, out_shape=(jax.ShapeDtypeStruct((LANES, TOK, WIDE)...  42.3 us
    pallas_call x1, Pallas kernels, on_device(): pl.pallas_call(finish, out_shape=(jax.ShapeDtypeStruct((TOK, QH * HD), BF...  2.51 us

profile of v5, /device:TPU:384, one launch (start us, length us, event | category | flops | bytes accessed | tf_op | source)
XLA Modules:
  0.0 45.4 jit_solution(14742695625781309509)
XLA Ops:
  0.6 42.3 %shard_map.84 = (bf16[4,128,512]{2,1,0:T(8,128)(2,1)}, bf16[4,128,512]{2,1,0:T(8,128)(2,1)}, bf16[8,2,128,128]{3,2,1,0:T(8,128)(2,1)}) custom-call(bf16[128,2048]{1,0:T(8,128)(2,1)} %q_hbm.1, bf16[128,512]{1,0:T(8,128)(2,1)} %k_hbm.1, bf16[128,512]{1,0:T(8,128)(2,1)} %v_hbm.1, bf16[128,2048]{1,0:T(8,128)(2,1)} %g_hbm.1, s32[1,128]{1,0:T(1,128)} %bitcast.1), custom_call_target="tpu_custom_call" | custom-call | tf_op jit(solution)/shard_map/pallas_call | solution.py:429
  42.9 2.5 %shard_map.85 = (bf16[128,2048]{1,0:T(8,128)(2,1)}, f32[128,2048]{1,0:T(8,128)}, f32[128,512]{1,0:T(8,128)}, f32[128,512]{1,0:T(8,128)}) custom-call(bf16[4,128,512]{2,1,0:T(8,128)(2,1)} %get-tuple-element.7.o_ref, bf16[4,128,512]{2,1,0:T(8,128)(2,1)} %get-tuple-element.8.dq_ref, bf16[8,2,128,128]{3,2,1,0:T(8,128)(2,1)} %get-tuple-element.9.dkv_ref), custom_call_target="tpu_custom_call" | custom-call | tf_op jit(solution)/shard_map/pallas_call | solution.py:474
